TPU v7x, 128 devices: a whole 4x4x4 slice. The times are simulated.
128 devices in a mesh: mem: 4 (over x), lat: 32 (over z, y, core).
Axes of the slice: x: 4, y: 4, z: 4, core: 2. Of those that a mesh axis runs over, the one named last changes fastest.
Arguments:
- prior_member_stack: float32 [64, 16, 256, 512], P('mem', None, 'lat'), may hold values from -6 to 6
- zonal_stability_ratio: float32 [256, 512], P('lat'), may hold values from -0.45 to 0.45
- meridional_stability_ratio: float32 [256, 512], P('lat'), may hold values from -0.45 to 0.45
- obs_perturb: bfloat16 [2048, 64, 4096], P(('mem', 'lat')), may hold values from -2 to 2
- innovation: float32 [2048, 4096], P(('mem', 'lat')), may hold values from -6 to 6
- inverse_error_variance: float32 [2048, 4096], P(('mem', 'lat')), may hold values from 0.25 to 4
- obs_count: int32 [2048], P(('mem', 'lat')), may hold values from 1 to 4096, 4194304 in all
- neighbours: int32 [2048, 6], P(('mem', 'lat')), may hold values from 0 to 47, as said below
- localization: float32 [2048, 6], P(('mem', 'lat')), may hold values from 0.2 to 1
Outputs:
- analysis: float32 [64, 16, 512, 256], P(None, None, ('mem', 'lat'))
Inputs may be any that keep to these rules, and one draw needn't show every extreme that they name: The observations of a tile fill its first obs_count slots; later slots are ignored. `neighbours`: window index w names row group w % 16 of the strip w // 16 - 1 places east (strips wrap around). Entry 0 of each row is the tile itself; the others are distinct tiles of the previous, same or next row group in the previous, same or next strip.
All inputs are finite; a program needn't handle non-finite values. No bound on the sum of `obs_count` on one device may be relied on, other than what follows from the above.
Results may differ from a plain program's by a relative error of at most 0.0022.
Values may be sent and summed in bfloat16 or wider, within the bound.
No kernel may reach another device: no remote copies, remote signals or barrier semaphores. Data moves between devices by JAX's collectives and lax.ppermute only.
A program may use at most 256 MiB of HBM per device.

v0:
```python
import jax
import jax.numpy as jnp
from jax import lax
from jax.sharding import PartitionSpec as P

NS_ITERS = 5


def extended(x, sides, width, wrap):
    for axis, dim in sides:
        size, length = (lax.axis_size(axis), x.shape[dim])
        up = [(i, (i + 1) % size) for i in range(size if wrap else size - 1)]
        down = [(j, i) for i, j in up]
        last = lax.slice_in_dim(x, length - width, length, axis=dim)
        leading = lax.slice_in_dim(x, 0, width, axis=dim)
        before = lax.ppermute(last, axis, up)
        after = lax.ppermute(leading, axis, down)
        x = jnp.concatenate([before, x, after], axis=dim)
    return x


def tile_terms(perturb, weight, drive):
    weighted = (perturb.astype(jnp.float32) * weight.astype(jnp.float32)[:, None, :]).astype(
        jnp.bfloat16
    )
    gram_matrix = jnp.einsum("tko,tlo->tkl", weighted, perturb, preferred_element_type=jnp.float32)
    drive_vector = jnp.einsum("tko,to->tk", perturb, drive, preferred_element_type=jnp.float32)
    return (gram_matrix, drive_vector)


def transform_weights(curvature, drive_total, members):
    frob_scale = jnp.sqrt(jnp.sum(curvature * curvature, axis=(1, 2)))
    identity = jnp.eye(members, dtype=jnp.float32)[None]
    current = curvature / frob_scale[:, None, None]
    inverse = jnp.broadcast_to(identity, curvature.shape)
    for _ in range(NS_ITERS):
        middle = 1.5 * identity - 0.5 * jnp.einsum(
            "tij,tjk->tik", inverse, current, precision=lax.Precision.HIGHEST
        )
        current = jnp.einsum("tij,tjk->tik", current, middle, precision=lax.Precision.HIGHEST)
        inverse = jnp.einsum("tij,tjk->tik", middle, inverse, precision=lax.Precision.HIGHEST)
    spread_part = jnp.sqrt((members - 1.0) / frob_scale)[:, None, None] * inverse
    half_step = jnp.einsum("tij,tj->ti", inverse, drive_total, precision=lax.Precision.HIGHEST)
    ensemble_mean_portion = (
        jnp.einsum("tij,tj->ti", inverse, half_step, precision=lax.Precision.HIGHEST)
        / frob_scale[:, None]
    )
    return spread_part + ensemble_mean_portion[:, :, None]


def per_device(
    prior_member_stack,
    zonal_stability_ratio,
    meridional_stability_ratio,
    obs_perturb,
    innovation,
    inverse_error_variance,
    obs_count,
    neighbours,
    localization,
):
    members_dev, channels, row_count, lon_count = prior_member_stack.shape
    mem_count = lax.axis_size("mem")
    lat_count = lax.axis_size("lat")
    lon_strip = lon_count // (mem_count * lat_count)
    members = members_dev * mem_count
    lat_total = row_count * lat_count
    east_neighbour = jnp.roll(prior_member_stack, -1, axis=-1)
    eastward_flux = (
        jnp.maximum(zonal_stability_ratio, 0.0) * prior_member_stack
        + jnp.minimum(zonal_stability_ratio, 0.0) * east_neighbour
    )
    divergence_x = eastward_flux - jnp.roll(eastward_flux, 1, axis=-1)
    stacked = jnp.concatenate(
        [
            prior_member_stack.reshape(members_dev * channels, row_count, lon_count),
            meridional_stability_ratio[None],
        ],
        axis=0,
    )
    padded = extended(stacked, (("lat", 1),), 1, False)
    fields_ext = padded[:-1].reshape(members_dev, channels, row_count + 2, lon_count)
    north_ext = padded[-1, :-1]
    flux_north = (
        jnp.maximum(north_ext, 0.0) * fields_ext[:, :, : row_count + 1]
        + jnp.minimum(north_ext, 0.0) * fields_ext[:, :, 1:]
    )
    transported_quantities = (
        prior_member_stack - divergence_x - (flux_north[:, :, 1:] - flux_north[:, :, :-1])
    )
    rows_last = jnp.swapaxes(transported_quantities, 2, 3)
    moved = rows_last.reshape(1, members_dev, channels, lon_count, row_count)
    arrived = lax.all_to_all(moved, ("mem", "lat"), split_axis=3, concat_axis=0, tiled=True)
    arrived = arrived.reshape(mem_count, lat_count, members_dev, channels, lon_strip, row_count)
    arrived = jnp.transpose(arrived, (0, 2, 3, 4, 1, 5)).reshape(
        members, channels, lon_strip, lat_total
    )
    blocks_per_processor, obs_cap = innovation.shape
    neigh_count = neighbours.shape[1]
    window_tiles = 3 * blocks_per_processor
    is_valid = (
        lax.broadcasted_iota(jnp.int32, (blocks_per_processor, obs_cap), 1) < obs_count[:, None]
    )
    obs_weight = jnp.where(is_valid, inverse_error_variance, 0.0).astype(jnp.bfloat16)
    obs_drive = jnp.where(is_valid, inverse_error_variance * innovation, 0.0).astype(jnp.bfloat16)
    window_slots = lax.broadcasted_iota(jnp.int32, (blocks_per_processor, window_tiles), 1)
    combine = jnp.zeros((blocks_per_processor, window_tiles), jnp.float32)
    for slot_index in range(neigh_count):
        combine = combine + jnp.where(
            neighbours[:, slot_index, None] == window_slots, localization[:, slot_index, None], 0.0
        )
    observed = jnp.concatenate([obs_perturb, obs_weight[:, None, :], obs_drive[:, None, :]], axis=1)
    received = extended(observed, ((("mem", "lat"), 0),), blocks_per_processor, True)
    gram_matrix, drive_vector = tile_terms(
        received[:, :members], received[:, members], received[:, members + 1]
    )
    window = jnp.concatenate([gram_matrix, drive_vector[:, None, :]], axis=1)
    gathered = jnp.einsum("ts,skl->tkl", combine, window, precision=lax.Precision.HIGHEST)
    curvature = (members - 1.0) * jnp.eye(members, dtype=jnp.float32)[None] + gathered[:, :members]
    drive_total = gathered[:, members]
    weights = transform_weights(curvature, drive_total, members)
    grid = arrived.reshape(
        members, channels, lon_strip, blocks_per_processor, lat_total // blocks_per_processor
    )
    member_mean = jnp.mean(grid, axis=0)
    anomaly = grid - member_mean
    update = jnp.einsum("icxtr,tij->jcxtr", anomaly, weights, precision=lax.Precision.HIGHEST)
    return (member_mean + update).reshape(members, channels, lon_strip, lat_total)


def solution(mesh):
    in_specs = (
        P("mem", None, "lat", None),
        P("lat", None),
        P("lat", None),
        P(("mem", "lat"), None, None),
        P(("mem", "lat"), None),
        P(("mem", "lat"), None),
        P(("mem", "lat")),
        P(("mem", "lat"), None),
        P(("mem", "lat"), None),
    )
    out_specs = P(None, None, ("mem", "lat"), None)
    return jax.shard_map(
        per_device, mesh=mesh, in_specs=in_specs, out_specs=out_specs, check_vma=False
    )
```

profile of v0, /device:TPU:0, one launch (start us, length us, event | category | flops | bytes accessed | tf_op | source)
XLA Modules:
  0.0 500.3 jit_solution(6737183816723738791)
XLA Ops:
  0.0 1.0 fusion.38
  1.0 1.1 fusion.39
  2.7 8.1 %pad_maximum_fusion.1 = bf16[16,66,4096]{2,1,0:T(8,128)(2,1)} fusion(bf16[16,1,4096]{2,1,0:T(2,128)(2,1)S(1)} %copy.224, bf16[16,1,4096]{2,1,0:T(2,128)(2,1)S(1)} %copy.223, bf16[16,64,4096]{2,1,0:T(8,128)(2,1)} %param.12), kind=kLoop, calls=%fused_computation.7 | loop fusion | flops 25952256 | bytes 17301504 | tf_op jit(solution)/shard_map/concatenate | solution.py:112
  10.8 11.8 %copy.225 = bf16[16,66,4096]{2,0,1:T(8,128)(2,1)} copy(bf16[16,66,4096]{2,1,0:T(8,128)(2,1)} %pad_maximum_fusion.1) | data formatting | bytes 17301504 | tf_op jit(solution)/shard_map/concatenate | solution.py:112
  22.6 8.2 %collective-permute-start.3 = (bf16[16,66,4096]{2,0,1:T(8,128)(2,1)}, bf16[16,66,4096]{2,0,1:T(8,128)(2,1)}, u32[]{:S(2)}, u32[]{:S(2)}) collective-permute-start(bf16[16,66,4096]{2,0,1:T(8,128)(2,1)} %copy.225), channel_id=1, source_target_pairs={{1,0},{2,1},{3,2},{4,3},{5,4},{6,5},{7,6},{8,7},{9,8},{10,9},{11,1... | collective-permute-start | bytes 25952264 | tf_op jit(solution)/shard_map/ppermute | solution.py:17
  30.8 3.9 fusion.27
  34.7 1.3 collective-permute-start.1
  36.0 3.3 collective-permute-start
  39.8 1.1 slice.92
  41.0 2.4 copy.213
  43.5 0.7 pad_maximum_fusion.5
  44.2 4.7 fusion.10
  49.4 0.8 pad_maximum_fusion.3
  50.3 1.2 fusion.6
  51.5 8.4 %fusion.8 = f32[1,16,16,512,8]{3,2,1,4,0:T(8,128)} fusion(f32[16,16,9,512]{3,1,0,2:T(8,128)S(1)} %fusion.6, f32[16,16,8,512]{3,1,0,2:T(8,128)S(1)} %fusion.10, f32[16,16,8,511]{3,1,0,2:T(8,128)S(1)} %bitcast.118, f32[16,16,8,1]{3,1,0,2:T(8,128)S(1)} %slice.121, f32[16,16,8,512]{3,2,1,0:T(8,128)S(1)} %copy-done), kind=kLoop, calls=%fused_computation.21 | loop fusion | flops 5242880 | bytes 25165824 | tf_op jit(solution)/shard_map/reshape | solution.py:92
  59.9 26.4 %copy.217 = f32[1,16,16,512,8]{2,4,1,0,3:T(8,128)} copy(f32[1,16,16,512,8]{3,2,1,4,0:T(8,128)} %fusion.8) | data formatting | bytes 8388608 | tf_op jit(solution)/shard_map/reshape | solution.py:92
  86.4 23.3 %reshape.89 = f32[128,1,8192]{2,1,0:T(1,128)} reshape(f32[512,1,16,8,16]{4,3,2,1,0:T(8,128)} %bitcast.114) | data formatting | bytes 8388608
  109.7 88.2 %all-to-all-start = ((f32[128,1,8192]{2,1,0:T(1,128)}), f32[128,1,8192]{2,1,0:T(1,128)}, u32[]{:S(2)}, u32[]{:S(2)}) async-start(f32[128,1,8192]{2,1,0:T(1,128)} %reshape.89), calls=%async_computation | async-start | bytes 8388608 | tf_op jit(solution)/shard_map/all_to_all | solution.py:93
  197.9 0.7 copy.232
  198.6 0.7 copy.231
  201.2 49.4 %all-to-all-done = f32[128,1,8192]{2,1,0:T(1,128)} async-done(((f32[128,1,8192]{2,1,0:T(1,128)}), f32[128,1,8192]{2,1,0:T(1,128)}, u32[]{:S(2)}, u32[]{:S(2)}) %all-to-all-start) | async-done | bytes 4194336 | tf_op jit(solution)/shard_map/all_to_all | solution.py:93
  251.1 13.9 %reduce.1 = f32[128,8192]{1,0:T(8,128)} reduce(f32[128,1,8192]{2,1,0:T(1,128)} %all-to-all-done, f32[]{:T(128)} %broadcast.80), dimensions={1}, to_apply=%all_to_all.11.reduce_sub_computation | reduce | bytes 8388612 | tf_op jit(solution)/shard_map/all_to_all | solution.py:93
  265.0 19.0 %reshape.90 = f32[512,1,16,8,16]{4,3,2,1,0:T(8,128)} reshape(f32[128,8192]{1,0:T(8,128)} %reduce.1) | data formatting | bytes 8388608
  284.0 41.8 %copy.219 = f32[4,32,16,16,4,8]{2,0,5,1,4,3:T(4,128)} copy(f32[4,32,16,16,4,8]{3,5,2,4,1,0:T(8,128)} %bitcast.115) | data formatting | bytes 8388608 | tf_op jit(solution)/shard_map/reshape | solution.py:94
  325.9 25.7 %reshape_reshape.3 = f32[64,16,4,16,16]{0,4,3,2,1:T(8,128)} reshape(f32[4,16,16,4,32,8]{1,0,5,4,3,2:T(4,128)} %bitcast.113) | data formatting | bytes 8388608 | tf_op jit(solution)/shard_map/reshape;reshape | solution.py:122
  351.6 28.7 %bitcast_reduce_fusion = f32[16,4,32,8]{3,2,1,0:T(8,128)S(1)} fusion(f32[4,32,16,16,4,8]{2,0,5,1,4,3:T(4,128)} %copy.219), kind=kLoop, calls=%fused_computation.131 | loop fusion | flops 1032192 | bytes 4259840 | tf_op jit(solution)/shard_map/reduce_sum | solution.py:125
  381.1 11.9 %copy.228 = bf16[16,66,4096]{2,1,0:T(8,128)(2,1)} copy(bf16[16,66,4096]{2,0,1:T(8,128)(2,1)} %collective-permute-done.3) | data formatting | bytes 17301504 | tf_op jit(solution)/shard_map/ppermute | solution.py:17
  393.0 11.9 %copy.227 = bf16[16,66,4096]{2,1,0:T(8,128)(2,1)} copy(bf16[16,66,4096]{2,0,1:T(8,128)(2,1)} %collective-permute-done.2) | data formatting | bytes 17301504 | tf_op jit(solution)/shard_map/ppermute | solution.py:16
  404.9 19.7 %pad_maximum_fusion = bf16[48,66,4096]{2,1,0:T(8,128)(2,1)} fusion(bf16[16,66,4096]{2,1,0:T(8,128)(2,1)} %copy.228, bf16[16,1,4096]{2,1,0:T(2,128)(2,1)S(1)} %copy.224, bf16[16,1,4096]{2,1,0:T(2,128)(2,1)S(1)} %copy.223, bf16[16,64,4096]{2,1,0:T(8,128)(2,1)} %param.12, bf16[16,66,4096]{2,1,0:T(8,128)(2,1)} %copy.227), kind=kLoop, calls=%fused_computation.2 | loop fusion | flops 129761280 | bytes 51904512 | tf_op jit(solution)/shard_map/concatenate | solution.py:18
  424.7 2.3 maximum_convert_fusion
  427.0 12.3 %fusion.3 = f32[48,1,64]{1,2,0:T(8,128)S(1)} fusion(bf16[48,66,4096]{2,1,0:T(8,128)(2,1)} %pad_maximum_fusion, bf16[16,66,4096]{2,1,0:T(8,128)(2,1)} %copy.228, bf16[16,66,4096]{2,1,0:T(8,128)(2,1)} %copy.227, bf16[16,1,4096]{2,1,0:T(2,128)(2,1)S(1)} %copy.224, bf16[16,1,4096]{2,1,0:T(2,128)(2,1)S(1)} %copy.223, bf16[16,64,4096]{2,1,0:T(8,128)(2,1)} %param.12), kind=kOutput, calls=%fused_computation.5 | convolution fusion | flops 27131904 | bytes 52703232 | tf_op jit(solution)/shard_map/broadcast_in_dim | solution.py:117
  439.4 1.4 copy.264
  440.8 18.9 %fusion = f32[48,64,64]{1,2,0:T(8,128)} fusion(f32[48,4096]{1,0:T(8,128)} %bitcast.122, bf16[48,66,4096]{2,1,0:T(8,128)(2,1)} %pad_maximum_fusion), kind=kOutput, calls=%fused_computation.1 | convolution fusion | flops 1648361472 | bytes 51904512 | tf_op jit(solution)/shard_map/tko,tlo->tkl/dot_general | solution.py:26
  459.8 1.9 pad_maximum_fusion.6
  461.8 1.7 fusion.12
  466.0 0.6 fusion.17
  467.9 0.6 fusion.16
  468.6 0.6 fusion.73
  469.2 0.6 fusion.74
  469.9 0.6 fusion.15
  471.2 0.6 fusion.76
  472.1 0.6 fusion.14
  472.7 0.9 fusion.77
  473.9 0.9 convolution_bitcast_fusion
  474.8 0.9 fusion.78
  475.8 11.8 %bitcast_add_fusion = f32[64,16,4,16,16]{0,4,2,1,3:T(8,128)S(1)} fusion(f32[64,16,4,16,16]{0,4,3,2,1:T(8,128)} %reshape_reshape.3, f32[16,4,16,16]{3,1,0,2:T(4,128)S(1)} %copy.222, f32[16,64,64]{2,1,0:T(8,128)S(1)} %fusion.77, f32[16,64]{1,0:T(8,128)S(1)} %broadcast_divide_fusion, f32[16]{0:T(128)S(1)} %get-tuple-element.23), kind=kOutput, calls=%fused_computation.8 | convolution fusion | flops 807534592 | bytes 8720448 | tf_op jit(solution)/shard_map/icxtr,tij->jcxtr/dot_general | solution.py:127
  487.6 4.3 copy.237
  491.9 7.9 %copy.238 = f32[64,16,4,256]{3,2,1,0:T(4,128)} copy(f32[64,16,4,256]{0,3,2,1:T(8,128)} %bitcast.120) | data formatting | bytes 8388608 | tf_op jit(solution)/shard_map/reshape | solution.py:128
  (79 shorter events, 9.8 us)
Async XLA Ops:
  10.8 20.0 %copy-start.4 = (f32[8,512]{1,0:T(8,128)S(1)}, f32[8,512]{1,0:T(8,128)}, u32[]{:S(2)}) copy-start(f32[8,512]{1,0:T(8,128)} %param.11) | copy-start | bytes 49156
  22.6 16.7 %copy-start = (f32[16,16,8,512]{3,2,1,0:T(8,128)S(1)}, f32[16,16,8,512]{3,2,1,0:T(8,128)}, u32[]{:S(2)}) copy-start(f32[16,16,8,512]{3,2,1,0:T(8,128)} %param.9) | copy-start | bytes 12582916
  22.6 358.5 %collective-permute-start.3 = (bf16[16,66,4096]{2,0,1:T(8,128)(2,1)}, bf16[16,66,4096]{2,0,1:T(8,128)(2,1)}, u32[]{:S(2)}, u32[]{:S(2)}) collective-permute-start(bf16[16,66,4096]{2,0,1:T(8,128)(2,1)} %copy.225), channel_id=1, source_target_pairs={{1,0},{2,1},{3,2},{4,3},{5,4},{6,5},{7,6},{8,7},{9,8},{10,9},{11,1... | collective-permute-start | bytes 25952264 | tf_op jit(solution)/shard_map/ppermute | solution.py:17
  30.8 362.2 %collective-permute-start.2 = (bf16[16,66,4096]{2,0,1:T(8,128)(2,1)}, bf16[16,66,4096]{2,0,1:T(8,128)(2,1)}, u32[]{:S(2)}, u32[]{:S(2)}) collective-permute-start(bf16[16,66,4096]{2,0,1:T(8,128)(2,1)} %copy.225), channel_id=1, source_target_pairs={{0,1},{1,2},{2,3},{3,4},{4,5},{5,6},{6,7},{7,8},{8,9},{9,10},{10,1... | collective-permute-start | bytes 25952264 | tf_op jit(solution)/shard_map/ppermute | solution.py:16
  34.7 14.6 %collective-permute-start.1 = (f32[257,1,512]{2,1,0:T(1,128)S(1)}, f32[257,1,512]{2,1,0:T(1,128)S(1)}, u32[]{:S(2)}, u32[]{:S(2)}) collective-permute-start(f32[257,1,512]{2,1,0:T(1,128)S(1)} %get-tuple-element.8), channel_id=1, source_target_pairs={{1,0},{2,1},{3,2},{4,3},{5,4},{6,5},{7,6},{8,7},{9,8},{10,9},{11,1... | collective-permute-start | bytes 1579016 | tf_op jit(solution)/shard_map/ppermute | solution.py:17
  36.0 13.4 %collective-permute-start = (f32[257,1,512]{2,1,0:T(1,128)S(1)}, f32[257,1,512]{2,1,0:T(1,128)S(1)}, u32[]{:S(2)}, u32[]{:S(2)}) collective-permute-start(f32[257,1,512]{2,1,0:T(1,128)S(1)} %get-tuple-element.7), channel_id=1, source_target_pairs={{0,1},{1,2},{2,3},{3,4},{4,5},{5,6},{6,7},{7,8},{8,9},{9,10},{10,1... | collective-permute-start | bytes 1579016 | tf_op jit(solution)/shard_map/ppermute | solution.py:16
  41.0 2.5 copy-start.5
  109.7 90.3 %copy-start.6 = (f32[16,6]{0,1:T(8,128)S(1)}, f32[16,6]{0,1:T(8,128)}, u32[]{:S(2)}) copy-start(f32[16,6]{0,1:T(8,128)} %param.17) | copy-start | bytes 1156
  109.7 90.9 %copy-start.7 = (s32[16,6]{0,1:T(8,128)S(1)}, s32[16,6]{0,1:T(8,128)}, u32[]{:S(2)}) copy-start(s32[16,6]{0,1:T(8,128)} %param.16) | copy-start | bytes 1156
  109.7 140.9 %all-to-all-start = ((f32[128,1,8192]{2,1,0:T(1,128)}), f32[128,1,8192]{2,1,0:T(1,128)}, u32[]{:S(2)}, u32[]{:S(2)}) async-start(f32[128,1,8192]{2,1,0:T(1,128)} %reshape.89), calls=%async_computation | async-start | bytes 8388608 | tf_op jit(solution)/shard_map/all_to_all | solution.py:93
  440.7 21.0 %copy-start.8 = (f32[16]{0:T(128)S(1)}, f32[16]{0:T(128)}, u32[]{:S(2)}) copy-start(f32[16]{0:T(128)} %get-tuple-element.17) | copy-start | bytes 196
  440.7 21.0 %copy-start.9 = (f32[16]{0:T(128)S(1)}, f32[16]{0:T(128)}, u32[]{:S(2)}) copy-start(f32[16]{0:T(128)} %get-tuple-element.18) | copy-start | bytes 196
  440.7 21.0 %copy-start.10 = (f32[16]{0:T(128)S(1)}, f32[16]{0:T(128)}, u32[]{:S(2)}) copy-start(f32[16]{0:T(128)} %get-tuple-element.19) | copy-start | bytes 196
  440.7 21.0 %copy-start.11 = (f32[16]{0:T(128)S(1)}, f32[16]{0:T(128)}, u32[]{:S(2)}) copy-start(f32[16]{0:T(128)} %get-tuple-element.20) | copy-start | bytes 196
  440.7 21.0 %copy-start.12 = (f32[16]{0:T(128)S(1)}, f32[16]{0:T(128)}, u32[]{:S(2)}) copy-start(f32[16]{0:T(128)} %get-tuple-element.21) | copy-start | bytes 196
  440.8 21.0 %copy-start.13 = (f32[16]{0:T(128)S(1)}, f32[16]{0:T(128)}, u32[]{:S(2)}) copy-start(f32[16]{0:T(128)} %get-tuple-element.22) | copy-start | bytes 196
  440.8 21.0 %copy-start.14 = (s32[16]{0:T(128)S(1)}, s32[16]{0:T(128)}, u32[]{:S(2)}) copy-start(s32[16]{0:T(128)} %get-tuple-element.11) | copy-start | bytes 196
  440.8 21.0 %copy-start.15 = (s32[16]{0:T(128)S(1)}, s32[16]{0:T(128)}, u32[]{:S(2)}) copy-start(s32[16]{0:T(128)} %get-tuple-element.12) | copy-start | bytes 196
  440.8 21.0 %copy-start.16 = (s32[16]{0:T(128)S(1)}, s32[16]{0:T(128)}, u32[]{:S(2)}) copy-start(s32[16]{0:T(128)} %get-tuple-element.13) | copy-start | bytes 196
  440.8 21.0 %copy-start.17 = (s32[16]{0:T(128)S(1)}, s32[16]{0:T(128)}, u32[]{:S(2)}) copy-start(s32[16]{0:T(128)} %get-tuple-element.14) | copy-start | bytes 196
  440.8 21.0 %copy-start.18 = (s32[16]{0:T(128)S(1)}, s32[16]{0:T(128)}, u32[]{:S(2)}) copy-start(s32[16]{0:T(128)} %get-tuple-element.15) | copy-start | bytes 196
  440.8 21.0 %copy-start.19 = (s32[16]{0:T(128)S(1)}, s32[16]{0:T(128)}, u32[]{:S(2)}) copy-start(s32[16]{0:T(128)} %get-tuple-element.16) | copy-start | bytes 196
  459.8 3.8 copy-start.3
  459.8 4.4 copy-start.1
  459.8 4.4 copy-start.2
where the time goes:
time: 509 us; the launch traced here: 500 us
  local copies, waits for them, and re-layouts  195 us (38%)
  starting transfers between devices  101 us (20%)
  other arithmetic  98.1 us (19%)
  matrix products  55.8 us (11%)
  waiting for transfers between devices  49.4 us (10%)
    all_to_all x1, starting transfers between devices, per_device(): lax.all_to_all(moved, ('mem', 'lat'), split_axis=3, concat_axis=0, tiled=...  88.2 us
    all_to_all x1, waiting for transfers between devices, per_device(): lax.all_to_all(moved, ('mem', 'lat'), split_axis=3, concat_axis=0, tiled=...  49.4 us
    unnamed x44, local copies, waits for them, and re-layouts  43.8 us
    reshape x1, local copies, waits for them, and re-layouts, per_device(): arrived.reshape(mem_count, lat_count, members_dev, channels, lon_strip, r...  41.8 us
    reduce_sum x1, other arithmetic, per_device(): member_mean = jnp.mean(grid, axis=0)  28.7 us
    reshape x1, local copies, waits for them, and re-layouts, per_device(): moved = rows_last.reshape(1, members_dev, channels, lon_count, row_count)  26.4 us
    another operation x1, local copies, waits for them, and re-layouts, per_device(): arrived.reshape(members, channels, lon_strip, blocks_per_processor, lat_t...  25.7 us
    concatenate x2, other arithmetic, extended(): x = jnp.concatenate([before, x, after], axis=dim)  20.5 us
  transfers between devices with their start and end apart: 5, of which 1 were waited for; matrix products, arithmetic and copies ran while one was open for 44% of the time, Pallas kernels for 0%

commit v1 on v0

v1 whole, which is shorter than its diff:
```python
import functools

import jax
import jax.numpy as jnp
from jax import lax
from jax.experimental import pallas as pl
from jax.experimental.pallas import tpu as pltpu
from jax.sharding import PartitionSpec as P

NS_ITERS = 5
LANES = 128
SUB = 8
VMEM_BYTES = 48 << 20


def call(kernel, name, out_shape, flops, traffic, **kw):
    return pl.pallas_call(
        kernel,
        name=name,
        out_shape=out_shape,
        cost_estimate=pl.CostEstimate(flops=flops, bytes_accessed=traffic, transcendentals=0),
        compiler_params=pltpu.CompilerParams(vmem_limit_bytes=VMEM_BYTES),
        **kw,
    )


def edge_rows(prior, north):
    rows, lon = prior.shape
    groups = rows // SUB

    def kernel(q_ref, v_ref, last_ref, first_ref):
        first_ref[...] = q_ref[pl.ds(0, groups, stride=SUB), :].astype(jnp.bfloat16)
        last_ref[0:groups, :] = q_ref[pl.ds(SUB - 1, groups, stride=SUB), :].astype(jnp.bfloat16)
        v = jnp.broadcast_to(v_ref[SUB - 1 : SUB, :], (16, LANES))
        high = v.astype(jnp.bfloat16).astype(jnp.float32)
        row = lax.broadcasted_iota(jnp.int32, (16, LANES), 0)
        parts = jnp.where(row == 0, high, jnp.where(row == 1, v - high, 0.0))
        last_ref[groups : groups + 16, :] = parts.astype(jnp.bfloat16)

    return call(
        kernel,
        "edge_rows",
        (
            jax.ShapeDtypeStruct((groups + 16, lon), jnp.bfloat16),
            jax.ShapeDtypeStruct((groups, lon), jnp.bfloat16),
        ),
        rows * lon,
        rows * lon * 4,
        grid=(lon // LANES,),
        in_specs=[
            pl.BlockSpec((rows, LANES), lambda s: (0, s)),
            pl.BlockSpec((SUB, LANES), lambda s: (0, s)),
        ],
        out_specs=(
            pl.BlockSpec((groups + 16, LANES), lambda s: (0, s)),
            pl.BlockSpec((groups, LANES), lambda s: (0, s)),
        ),
    )(prior, north)


def advect(prior, zonal, north, south_rows, north_rows, turn):
    members, channels, sub, lon = prior.shape
    steps = 4
    per_step = members // steps
    width = channels * sub
    blocks = lon // LANES

    def kernel(
        turn_ref, q_ref, u_ref, v_ref, vs_ref, hs_ref, hn_ref, out_ref, coef_ref, adv_ref, rows_ref
    ):
        step = pl.program_id(0)

        @pl.when(step == 0)
        def _():
            u, v = u_ref[...], v_ref[...]
            row = lax.broadcasted_iota(jnp.int32, (sub, lon), 0)
            below = vs_ref[0:1, :].astype(jnp.float32) + vs_ref[1:2, :].astype(jnp.float32)
            v_south = jnp.where(row == 0, jnp.broadcast_to(below, (sub, lon)), pltpu.roll(v, 1, 0))
            u_west = pltpu.roll(u, 1, 1)
            vp, vn = jnp.maximum(v, 0.0), jnp.minimum(v, 0.0)
            vps, vns = jnp.maximum(v_south, 0.0), jnp.minimum(v_south, 0.0)
            coef_ref[0] = (
                1.0 - jnp.maximum(u, 0.0) + jnp.minimum(u_west, 0.0) - vp + vns
            )
            coef_ref[1] = -jnp.minimum(u, 0.0)
            coef_ref[2] = jnp.maximum(u_west, 0.0)
            coef_ref[3] = jnp.where(row == sub - 1, 0.0, -vn)
            coef_ref[4] = jnp.where(row == 0, 0.0, vps)
            coef_ref[5] = jnp.broadcast_to(vps[0:1], (sub, lon))
            coef_ref[6] = jnp.broadcast_to(-vn[sub - 1 : sub], (sub, lon))

        shift = turn_ref[0] * sub
        for k in range(per_step):
            member = step * per_step + k
            for c in range(channels):
                q = q_ref[k, c]
                moved = (
                    q * coef_ref[0]
                    + pltpu.roll(q, lon - 1, 1) * coef_ref[1]
                    + pltpu.roll(q, 1, 1) * coef_ref[2]
                    + pltpu.roll(q, sub - 1, 0) * coef_ref[3]
                    + pltpu.roll(q, 1, 0) * coef_ref[4]
                )
                for b in range(blocks):
                    adv_ref[b, c * sub : (c + 1) * sub, :] = moved[:, b * LANES : (b + 1) * LANES]
            at = pl.ds(pl.multiple_of(k * channels, channels), channels)
            low = pl.ds(0, channels, stride=sub)
            high = pl.ds(sub - 1, channels, stride=sub)
            hs, hn = hs_ref[at, :].astype(jnp.float32), hn_ref[at, :].astype(jnp.float32)
            hs, hn = hs * coef_ref[5, 0:1], hn * coef_ref[6, 0:1]
            for b in range(blocks):
                lane = slice(b * LANES, (b + 1) * LANES)
                adv_ref[b, low, :] = adv_ref[b, low, :] + hs[:, lane]
                adv_ref[b, high, :] = adv_ref[b, high, :] + hn[:, lane]
                turned = pltpu.roll(adv_ref[b].T, shift, 1)
                rows_ref[pl.ds(b * LANES * members + member, LANES, stride=members), :] = turned

        @pl.when(step == steps - 1)
        def _():
            @pl.loop(0, lon // 32)
            def _(i):
                at = pl.ds(pl.multiple_of(i * 32 * members, 32 * members), 32 * members)
                out_ref[at, :] = rows_ref[at, :].astype(jnp.bfloat16)

    cells = members * channels * sub * lon
    return call(
        kernel,
        "advect",
        jax.ShapeDtypeStruct((lon * members, width), jnp.bfloat16),
        cells * 10,
        cells * 6,
        grid=(steps,),
        in_specs=[
            pl.BlockSpec(memory_space=pltpu.SMEM),
            pl.BlockSpec((per_step, channels, sub, lon), lambda s: (s, 0, 0, 0)),
            pl.BlockSpec((sub, lon), lambda s: (0, 0)),
            pl.BlockSpec((sub, lon), lambda s: (0, 0)),
            pl.BlockSpec((16, lon), lambda s: (members, 0)),
            pl.BlockSpec((per_step * channels, lon), lambda s: (s, 0)),
            pl.BlockSpec((per_step * channels, lon), lambda s: (s, 0)),
        ],
        out_specs=pl.BlockSpec((lon * members, width), lambda s: (0, 0)),
        scratch_shapes=[
            pltpu.VMEM((7, sub, lon), jnp.float32),
            pltpu.VMEM((blocks, width, LANES), jnp.float32),
            pltpu.VMEM((lon * members, width), jnp.float32),
        ],
    )(turn, prior, zonal, north, south_rows, south_rows, north_rows)


def tile_sums(perturb, innovation, inverse_error_variance, obs_count):
    tiles, members, cap = perturb.shape
    steps = 4
    per_step = tiles // steps
    half = members // 2

    def kernel(count_ref, p_ref, inn_ref, iev_ref, out_ref):
        step = pl.program_id(0)
        slot = lax.broadcasted_iota(jnp.int32, (1, cap), 1)
        for k in range(per_step):
            tile = step * per_step + k
            valid = slot < count_ref[tile]
            iev = iev_ref[pl.ds(tile, 1), :]
            weight = jnp.where(valid, iev, 0.0)
            drive = jnp.where(valid, iev * inn_ref[pl.ds(tile, 1), :], 0.0)
            weight = jnp.broadcast_to(weight, (16, cap)).astype(jnp.bfloat16)
            drive = jnp.broadcast_to(drive, (16, cap)).astype(jnp.bfloat16)
            p = p_ref[k]
            left = jnp.concatenate(
                [p[i * 16 : (i + 1) * 16] * weight for i in range(members // 16)] + [drive], axis=0
            )
            sums = lax.dot_general(
                left, p, (((1,), (1,)), ((), ())), preferred_element_type=jnp.float32
            )
            out_ref[k, 0:half, :] = jnp.concatenate([sums[0:half], sums[half:members]], axis=1)
            last = sums[members : members + SUB]
            out_ref[k, half : half + SUB, :] = jnp.concatenate([last, last], axis=1)

    return call(
        kernel,
        "tile_sums",
        jax.ShapeDtypeStruct((tiles, half + SUB, 2 * members), jnp.float32),
        2 * tiles * members * (members + 16) * cap,
        tiles * members * cap * 2,
        grid=(steps,),
        in_specs=[
            pl.BlockSpec(memory_space=pltpu.SMEM),
            pl.BlockSpec((per_step, members, cap), lambda s: (s, 0, 0)),
            pl.BlockSpec((tiles, cap), lambda s: (0, 0)),
            pl.BlockSpec((tiles, cap), lambda s: (0, 0)),
        ],
        out_specs=pl.BlockSpec((per_step, half + SUB, 2 * members), lambda s: (s, 0, 0)),
    )(obs_count, perturb, innovation, inverse_error_variance)


def transform(west, own, east, neighbours, localization):
    tiles, packed, lanes = own.shape
    members = lanes // 2
    half = members // 2
    neigh = neighbours.shape[1]
    dot = functools.partial(
        jnp.dot, precision=lax.Precision.HIGHEST, preferred_element_type=jnp.float32
    )

    def kernel(nb_ref, loc_ref, w_ref, o_ref, e_ref, out_ref, win_ref, cur_ref, inv_ref, mid_ref):
        win_ref[0:tiles] = w_ref[...]
        win_ref[tiles : 2 * tiles] = o_ref[...]
        win_ref[2 * tiles : 3 * tiles] = e_ref[...]
        row = lax.broadcasted_iota(jnp.int32, (members, members), 0)
        col = lax.broadcasted_iota(jnp.int32, (members, members), 1)
        eye = (row == col).astype(jnp.float32)
        drives, scales = [], []
        for t in range(tiles):
            total = loc_ref[t, 0] * win_ref[nb_ref[t, 0]]
            for n in range(1, neigh):
                total = total + loc_ref[t, n] * win_ref[nb_ref[t, n]]
            curvature = (members - 1.0) * eye + jnp.concatenate(
                [total[0:half, 0:members], total[0:half, members:]], axis=0
            )
            drives.append(total[half : half + SUB, 0:members])
            square = jnp.sum(curvature * curvature, axis=0, keepdims=True)
            scale = jnp.sqrt(jnp.sum(square, axis=1, keepdims=True))
            scales.append(scale)
            cur_ref[t] = curvature / scale
        for step in range(NS_ITERS):
            for t in range(tiles):
                product = cur_ref[t] if step == 0 else dot(inv_ref[t], cur_ref[t])
                mid_ref[t] = 1.5 * eye - 0.5 * product
            for t in range(tiles):
                middle = mid_ref[t]
                if step < NS_ITERS - 1:
                    cur_ref[t] = dot(cur_ref[t], middle)
                inv_ref[t] = middle if step == 0 else dot(middle, inv_ref[t])
        for t in range(tiles):
            flipped = inv_ref[t].T
            half_step = dot(drives[t], flipped)
            mean_part = dot(half_step, flipped)[0:1] / scales[t]
            weights = jnp.sqrt((members - 1.0) / scales[t]) * flipped + mean_part
            rest = (1.0 - jnp.sum(weights, axis=1, keepdims=True)) * (1.0 / members)
            weights = weights + rest
            high = weights.astype(jnp.bfloat16).astype(jnp.float32)
            out_ref[t] = jnp.concatenate([high, weights - high], axis=1).astype(jnp.bfloat16)

    cube = pltpu.VMEM((tiles, members, members), jnp.float32)
    vmem = pl.BlockSpec(memory_space=pltpu.VMEM)
    smem = pl.BlockSpec(memory_space=pltpu.SMEM)
    return call(
        kernel,
        "transform",
        jax.ShapeDtypeStruct((tiles, members, lanes), jnp.bfloat16),
        2 * tiles * members**3 * 72,
        tiles * packed * lanes * 12,
        in_specs=[smem, smem, vmem, vmem, vmem],
        out_specs=vmem,
        scratch_shapes=[pltpu.VMEM((3 * tiles, packed, lanes), jnp.float32), cube, cube, cube],
    )(neighbours, localization, west, own, east)


def analyse(arrived, weights, mem_count, lat_count, lon_strip):
    sources, rows, lanes = arrived.shape
    members_dev = rows // lon_strip
    tiles, members, _ = weights.shape
    bands = lat_count // tiles
    group = lanes // SUB
    halves = lat_count // group
    per_member = group * halves * lon_strip

    def kernel(a_ref, w_ref, out_ref, product_ref):
        x = pl.program_id(0)
        for g in range(tiles):
            block = jnp.concatenate(
                [
                    jnp.concatenate(
                        [a_ref[m * lat_count + g * bands + b] for m in range(mem_count)], axis=0
                    )
                    for b in range(bands)
                ],
                axis=1,
            )
            product = jnp.dot(
                w_ref[g],
                jnp.concatenate([block, block], axis=0),
                preferred_element_type=jnp.float32,
            )
            for b in range(bands):
                product_ref[g * bands + b] = product[:, b * lanes : (b + 1) * lanes]
        place = lax.broadcasted_iota(jnp.int32, (SUB, lanes), 1) // SUB

        @pl.loop(0, members // SUB)
        def _(j):
            at = pl.ds(pl.multiple_of(j * SUB, SUB), SUB)
            for half in range(halves):
                held = [product_ref[half * group + b, at, :] for b in range(group)]
                step = 1
                while step < group:
                    odd = (place // step) % 2 == 1
                    held = [
                        jnp.where(odd, held[(r + step) % group], held[r]) for r in range(group)
                    ]
                    step *= 2
                for c in range(group):
                    row = pltpu.roll(held[(-c) % group], (lanes - c * SUB) % lanes, 1)
                    first = j * SUB * per_member + (c * halves + half) * lon_strip + x
                    out_ref[pl.ds(first, SUB, stride=per_member), :] = row

    return call(
        kernel,
        "analyse",
        jax.ShapeDtypeStruct((members * per_member, lanes), jnp.float32),
        2 * tiles * members * 2 * members * bands * lanes * lon_strip,
        members * per_member * lanes * 6,
        grid=(lon_strip,),
        in_specs=[
            pl.BlockSpec((sources, members_dev, lanes), lambda x: (0, x, 0)),
            pl.BlockSpec((tiles, members, 2 * members), lambda x: (0, 0, 0)),
        ],
        out_specs=pl.BlockSpec((members * per_member, lanes), lambda x: (0, 0)),
        scratch_shapes=[pltpu.VMEM((lat_count, members, lanes), jnp.float32)],
    )(arrived, weights)


def per_device(
    prior_member_stack,
    zonal_stability_ratio,
    meridional_stability_ratio,
    obs_perturb,
    innovation,
    inverse_error_variance,
    obs_count,
    neighbours,
    localization,
):
    members_dev, channels, row_count, lon_count = prior_member_stack.shape
    mem_count, lat_count = lax.axis_size("mem"), lax.axis_size("lat")
    devices = mem_count * lat_count
    lon_strip = lon_count // devices
    members = members_dev * mem_count

    last, first = edge_rows(
        prior_member_stack.reshape(members_dev * channels * row_count, lon_count),
        meridional_stability_ratio,
    )
    up = [(i, i + 1) for i in range(lat_count - 1)]
    down = [(j, i) for i, j in up]
    south_rows = lax.ppermute(last, "lat", up)
    north_rows = lax.ppermute(first, "lat", down)

    sums = tile_sums(obs_perturb, innovation, inverse_error_variance, obs_count)
    ring = [(i, (i + 1) % devices) for i in range(devices)]
    both = ("mem", "lat")
    west = lax.ppermute(sums, both, ring)
    east = lax.ppermute(sums, both, [(j, i) for i, j in ring])

    turn = (lax.axis_index("lat") % (LANES // SUB)).astype(jnp.int32).reshape(1)
    sent = advect(
        prior_member_stack,
        zonal_stability_ratio,
        meridional_stability_ratio,
        south_rows,
        north_rows,
        turn,
    )
    sent = sent.reshape(devices, lon_strip * members_dev, channels * row_count)
    arrived = lax.all_to_all(sent, both, split_axis=0, concat_axis=0, tiled=True)
    weights = transform(west, sums, east, neighbours, localization)
    rows = analyse(arrived, weights, mem_count, lat_count, lon_strip)
    halves = lat_count * row_count // LANES
    out = rows.reshape(members, channels, halves, lon_strip, LANES)
    out = jnp.transpose(out, (0, 1, 3, 2, 4))
    return out.reshape(members, channels, lon_strip, lat_count * row_count)


def solution(mesh):
    in_specs = (
        P("mem", None, "lat", None),
        P("lat", None),
        P("lat", None),
        P(("mem", "lat"), None, None),
        P(("mem", "lat"), None),
        P(("mem", "lat"), None),
        P(("mem", "lat")),
        P(("mem", "lat"), None),
        P(("mem", "lat"), None),
    )
    out_specs = P(None, None, ("mem", "lat"), None)
    return jax.shard_map(
        per_device, mesh=mesh, in_specs=in_specs, out_specs=out_specs, check_vma=False
    )
```

time: 509 us -> 87.7 us (0.17); the launches traced: 500 us -> 87.3 us
  local copies, waits for them, and re-layouts: 195 us -> 4.42 us
  other arithmetic: 98.1 us -> 0 us
  starting transfers between devices: 101 us -> 26.6 us
  matrix products: 55.8 us -> 0 us
  Pallas kernels: 0 us -> 31.7 us
  waiting for transfers between devices: 49.4 us -> 24.5 us
    reshape x3 -> x0, local copies, waits for them, and re-layouts: 76.2 us -> none  [the longest x1 41.8 us: per_device(): arrived.reshape(mem_count, lat_count, members_dev, channels, lon_strip, r...]
    all_to_all x1, starting transfers between devices: 88.2 us -> 16.9 us  [per_device(): lax.all_to_all(sent, both, split_axis=0, concat_axis=0, tiled=True)]
    all_to_all x1, waiting for transfers between devices: 49.4 us -> 0.01 us  [per_device(): lax.all_to_all(sent, both, split_axis=0, concat_axis=0, tiled=True)]
    dot_general x19 -> x0, matrix products: 43.5 us -> none  [the longest x1 18.9 us: tile_terms(): jnp.einsum('tko,tlo->tkl', weighted, perturb, preferred_element_type=jnp....]
    unnamed x44 -> x22, local copies, waits for them, and re-layouts: 43.8 us -> 4.42 us
    concatenate x7 -> x0, other arithmetic: 35.6 us -> none  [the longest x2 20.5 us: extended(): x = jnp.concatenate([before, x, after], axis=dim)]
    pallas_call x0 -> x5, Pallas kernels: none -> 31.7 us  [the longest x1 8.74 us: advect(): call(kernel, 'advect', jax.ShapeDtypeStruct((lon * members, width), jnp.b...]
    reduce_sum x2 -> x0, other arithmetic: 28.9 us -> none  [the longest x1 28.7 us: per_device(): member_mean = jnp.mean(grid, axis=0)]
  transfers between devices with their start and end apart: 5 -> 5, of which waited for: 1 -> 3; matrix products, arithmetic and copies ran while one was open for 44% -> 0% of each run, Pallas kernels for 0% -> 16%
where the time goes in v1:
time: 87.7 us; the launch traced here: 87.3 us
  Pallas kernels  31.7 us (36%)
  starting transfers between devices  26.6 us (30%)
  waiting for transfers between devices  24.5 us (28%)
  local copies, waits for them, and re-layouts  4.42 us (5%)
    all_to_all x1, starting transfers between devices, per_device(): lax.all_to_all(sent, both, split_axis=0, concat_axis=0, tiled=True)  16.9 us
    ppermute x1, waiting for transfers between devices, per_device(): east = lax.ppermute(sums, both, [(j, i) for i, j in ring])  12.2 us
    pallas_call x1, Pallas kernels, advect(): call(kernel, 'advect', jax.ShapeDtypeStruct((lon * members, width), jnp.b...  8.74 us
    ppermute x1, waiting for transfers between devices, per_device(): west = lax.ppermute(sums, both, ring)  8.27 us
    pallas_call x1, Pallas kernels, analyse(): call(kernel, 'analyse', jax.ShapeDtypeStruct((members * per_member, lanes...  8.25 us
    pallas_call x1, Pallas kernels, transform(): call(kernel, 'transform', jax.ShapeDtypeStruct((tiles, members, lanes), j...  7.62 us
    ppermute x1, starting transfers between devices, per_device(): east = lax.ppermute(sums, both, [(j, i) for i, j in ring])  7.12 us
    pallas_call x1, Pallas kernels, tile_sums(): call(kernel, 'tile_sums', jax.ShapeDtypeStruct((tiles, half + SUB, 2 * me...  6.11 us
  transfers between devices with their start and end apart: 5, of which 3 were waited for; matrix products, arithmetic and copies ran while one was open for 0% of the time, Pallas kernels for 16%

profile of v1, /device:TPU:0, one launch (start us, length us, event | category | flops | bytes accessed | tf_op | source)
XLA Modules:
  0.0 87.3 jit_solution(506340547595819451)
XLA Ops:
  0.0 0.0 copy-start
  0.0 2.2 %copy-done = f32[16,16,8,512]{3,2,1,0:T(8,128)S(1)} copy-done((f32[16,16,8,512]{3,2,1,0:T(8,128)S(1)}, f32[16,16,8,512]{3,2,1,0:T(8,128)}, u32[]{:S(2)}) %copy-start) | copy-done | bytes 4194328
  2.2 0.0 copy-start.4
  2.2 0.7 copy-done.4
  2.9 0.0 copy-start.5
  2.9 0.0 copy-start.6
  2.9 0.9 %edge_rows.1 = (bf16[272,512]{1,0:T(8,128)(2,1)S(1)}, bf16[256,512]{1,0:T(8,128)(2,1)S(1)}) custom-call(f32[2048,512]{1,0:T(8,128)S(1)} %bitcast.8, f32[8,512]{1,0:T(8,128)S(1)} %copy-done.4), custom_call_target="tpu_custom_call" | custom-call | flops 1048576 | bytes 4194304 | tf_op jit(solution)/shard_map/edge_rows/pallas_call | solution.py:40
  3.9 1.3 %collective-permute-start = (bf16[272,512]{1,0:T(8,128)(2,1)S(1)}, bf16[272,512]{1,0:T(8,128)(2,1)S(1)}, u32[]{:S(2)}, u32[]{:S(2)}) collective-permute-start(bf16[272,512]{1,0:T(8,128)(2,1)S(1)} %get-tuple-element.7), channel_id=1, source_target_pairs={{0,1},{1,2},{2,3},{3,4},{4,5},{5,6},{6,7},{7,8},{8,9},{9,10},{10,1... | collective-permute-start | bytes 835592 | tf_op jit(solution)/shard_map/ppermute | solution.py:345
  5.2 1.3 %collective-permute-start.1 = (bf16[256,512]{1,0:T(8,128)(2,1)S(1)}, bf16[256,512]{1,0:T(8,128)(2,1)S(1)}, u32[]{:S(2)}, u32[]{:S(2)}) collective-permute-start(bf16[256,512]{1,0:T(8,128)(2,1)S(1)} %get-tuple-element.8), channel_id=1, source_target_pairs={{1,0},{2,1},{3,2},{4,3},{5,4},{6,5},{7,6},{8,7},{9,8},{10,9},{11,1... | collective-permute-start | bytes 786440 | tf_op jit(solution)/shard_map/ppermute | solution.py:346
  6.5 4.0 %collective-permute-done.1.hn_ref = bf16[256,512]{1,0:T(8,128)(2,1)S(1)} collective-permute-done((bf16[256,512]{1,0:T(8,128)(2,1)S(1)}, bf16[256,512]{1,0:T(8,128)(2,1)S(1)}, u32[]{:S(2)}, u32[]{:S(2)}) %collective-permute-start.1) | collective-permute-done | bytes 262176 | tf_op jit(solution)/shard_map/ppermute | solution.py:346
  10.5 0.0 collective-permute-done.vs_ref.hs_ref
  10.5 0.0 copy-done.5
  10.5 0.0 copy-done.6
  10.5 0.0 copy-start.2
  10.5 0.0 copy-start.3
  10.5 0.0 copy-start.7
  10.5 8.7 %advect.1 = bf16[8192,128]{1,0:T(8,128)(2,1)S(1)} custom-call(s32[1]{0:T(128)} %bitcast.turn_ref, f32[16,16,8,512]{3,2,1,0:T(8,128)} %q_ref.1, f32[8,512]{1,0:T(8,128)S(1)} %copy-done.6, f32[8,512]{1,0:T(8,128)S(1)} %copy-done.5, bf16[272,512]{1,0:T(8,128)(2,1)S(1)} %collective-permute-done.vs_ref.hs_ref, ...), custom_call_target="tpu_custom_call" | custom-call | flops 10485760 | bytes 6291456 | tf_op jit(solution)/shard_map/advect/pallas_call | solution.py:126
  19.3 0.0 copy-start.1
  19.3 1.3 %copy-done.1 = bf16[8192,128]{1,0:T(8,128)(2,1)} copy-done((bf16[8192,128]{1,0:T(8,128)(2,1)}, bf16[8192,128]{1,0:T(8,128)(2,1)S(1)}, u32[]{:S(2)}) %copy-start.1) | copy-done | bytes 2097176
  20.6 16.9 %all-to-all-start = ((bf16[128,64,128]{2,1,0:T(8,128)(2,1)}), bf16[128,64,128]{2,1,0:T(8,128)(2,1)S(1)}, u32[]{:S(2)}, u32[]{:S(2)}) async-start(bf16[128,64,128]{2,1,0:T(8,128)(2,1)} %bitcast.9), calls=%async_computation | async-start | bytes 4194304 | tf_op jit(solution)/shard_map/all_to_all | solution.py:364
  37.5 0.0 copy-done.2
  37.5 0.0 copy-done.3
  37.5 0.0 copy-done.7
  37.5 0.0 copy-start.8
  37.5 0.0 copy-start.9
  37.5 6.1 %tile_sums.1.o_ref = f32[16,40,128]{2,1,0:T(8,128)S(1)} custom-call(s32[16]{0:T(128)S(1)} %copy-done.7, bf16[16,64,4096]{2,1,0:T(8,128)(2,1)} %p_ref.1, f32[16,4096]{1,0:T(8,128)S(1)} %copy-done.2, f32[16,4096]{1,0:T(8,128)S(1)} %copy-done.3), custom_call_target="tpu_custom_call" | custom-call | flops 671088640 | bytes 8388608 | tf_op jit(solution)/shard_map/tile_sums/pallas_call | solution.py:179
  43.7 7.1 %collective-permute-start.3 = (f32[16,40,128]{2,1,0:T(8,128)S(1)}, f32[16,40,128]{2,1,0:T(8,128)S(1)}, u32[]{:S(2)}, u32[]{:S(2)}) collective-permute-start(f32[16,40,128]{2,1,0:T(8,128)S(1)} %tile_sums.1.o_ref), channel_id=1, source_target_pairs={{1,0},{2,1},{3,2},{4,3},{5,4},{6,5},{7,6},{8,7},{9,8},{10,9},{11,1... | collective-permute-start | bytes 983048 | tf_op jit(solution)/shard_map/ppermute | solution.py:352
  50.8 0.0 collective-permute-start.2
  50.8 0.0 copy-done.8
  50.8 0.1 copy.10.nb_ref
  50.9 0.0 copy-done.9
  50.9 0.1 copy.11.loc_ref
  51.0 12.2 %collective-permute-done.3.e_ref = f32[16,40,128]{2,1,0:T(8,128)S(1)} collective-permute-done((f32[16,40,128]{2,1,0:T(8,128)S(1)}, f32[16,40,128]{2,1,0:T(8,128)S(1)}, u32[]{:S(2)}, u32[]{:S(2)}) %collective-permute-start.3) | collective-permute-done | bytes 327712 | tf_op jit(solution)/shard_map/ppermute | solution.py:352
  63.2 8.3 %collective-permute-done.2.w_ref = f32[16,40,128]{2,1,0:T(8,128)S(1)} collective-permute-done((f32[16,40,128]{2,1,0:T(8,128)S(1)}, f32[16,40,128]{2,1,0:T(8,128)S(1)}, u32[]{:S(2)}, u32[]{:S(2)}) %collective-permute-start.2) | collective-permute-done | bytes 327712 | tf_op jit(solution)/shard_map/ppermute | solution.py:351
  71.4 7.6 %transform.1.w_ref = bf16[16,64,128]{2,1,0:T(8,128)(2,1)S(1)} custom-call(s32[16,6]{1,0:T(8,128)S(1)} %copy.10.nb_ref, f32[16,6]{1,0:T(8,128)S(1)} %copy.11.loc_ref, f32[16,40,128]{2,1,0:T(8,128)S(1)} %collective-permute-done.2.w_ref, f32[16,40,128]{2,1,0:T(8,128)S(1)} %tile_sums.1.o_ref, f32[16,40,128]{2,1,0:T(8,128)S(1)} %collective-permute-done.3.e_ref), custom_call_target="tpu_custom_call" | custom-call | flops 603979776 | bytes 983040 | tf_op jit(solution)/shard_map/transform/pallas_call | solution.py:247
  79.1 0.0 all-to-all-done.a_ref
  79.1 8.2 %analyse.1 = f32[8192,128]{1,0:T(8,128)} custom-call(bf16[128,64,128]{2,1,0:T(8,128)(2,1)S(1)} %all-to-all-done.a_ref, bf16[16,64,128]{2,1,0:T(8,128)(2,1)S(1)} %transform.1.w_ref), custom_call_target="tpu_custom_call" | custom-call | flops 268435456 | bytes 6291456 | tf_op jit(solution)/shard_map/analyse/pallas_call | solution.py:306
Async XLA Ops:
  0.0 2.2 %copy-start = (f32[16,16,8,512]{3,2,1,0:T(8,128)S(1)}, f32[16,16,8,512]{3,2,1,0:T(8,128)}, u32[]{:S(2)}) copy-start(f32[16,16,8,512]{3,2,1,0:T(8,128)} %q_ref.1) | copy-start | bytes 12582916
  2.2 0.7 copy-start.4
  2.9 7.6 %copy-start.5 = (f32[8,512]{1,0:T(8,128)S(1)}, f32[8,512]{1,0:T(8,128)}, u32[]{:S(2)}) copy-start(f32[8,512]{1,0:T(8,128)} %v_ref.3) | copy-start | bytes 49156
  2.9 7.6 %copy-start.6 = (f32[8,512]{1,0:T(8,128)S(1)}, f32[8,512]{1,0:T(8,128)}, u32[]{:S(2)}) copy-start(f32[8,512]{1,0:T(8,128)} %u_ref.1) | copy-start | bytes 49156
  3.9 6.6 %collective-permute-start = (bf16[272,512]{1,0:T(8,128)(2,1)S(1)}, bf16[272,512]{1,0:T(8,128)(2,1)S(1)}, u32[]{:S(2)}, u32[]{:S(2)}) collective-permute-start(bf16[272,512]{1,0:T(8,128)(2,1)S(1)} %get-tuple-element.7), channel_id=1, source_target_pairs={{0,1},{1,2},{2,3},{3,4},{4,5},{5,6},{6,7},{7,8},{8,9},{9,10},{10,1... | collective-permute-start | bytes 835592 | tf_op jit(solution)/shard_map/ppermute | solution.py:345
  5.2 5.3 %collective-permute-start.1 = (bf16[256,512]{1,0:T(8,128)(2,1)S(1)}, bf16[256,512]{1,0:T(8,128)(2,1)S(1)}, u32[]{:S(2)}, u32[]{:S(2)}) collective-permute-start(bf16[256,512]{1,0:T(8,128)(2,1)S(1)} %get-tuple-element.8), channel_id=1, source_target_pairs={{1,0},{2,1},{3,2},{4,3},{5,4},{6,5},{7,6},{8,7},{9,8},{10,9},{11,1... | collective-permute-start | bytes 786440 | tf_op jit(solution)/shard_map/ppermute | solution.py:346
  10.5 27.0 %copy-start.2 = (f32[16,4096]{1,0:T(8,128)S(1)}, f32[16,4096]{1,0:T(8,128)}, u32[]{:S(2)}) copy-start(f32[16,4096]{1,0:T(8,128)} %inn_ref.1) | copy-start | bytes 786436
  10.5 27.0 %copy-start.3 = (f32[16,4096]{1,0:T(8,128)S(1)}, f32[16,4096]{1,0:T(8,128)}, u32[]{:S(2)}) copy-start(f32[16,4096]{1,0:T(8,128)} %iev_ref.1) | copy-start | bytes 786436
  10.5 27.0 %copy-start.7 = (s32[16]{0:T(128)S(1)}, s32[16]{0:T(128)}, u32[]{:S(2)}) copy-start(s32[16]{0:T(128)} %count_ref.1) | copy-start | bytes 196
  19.3 1.3 %copy-start.1 = (bf16[8192,128]{1,0:T(8,128)(2,1)}, bf16[8192,128]{1,0:T(8,128)(2,1)S(1)}, u32[]{:S(2)}) copy-start(bf16[8192,128]{1,0:T(8,128)(2,1)S(1)} %advect.1) | copy-start | bytes 6291460
  20.6 58.5 %all-to-all-start = ((bf16[128,64,128]{2,1,0:T(8,128)(2,1)}), bf16[128,64,128]{2,1,0:T(8,128)(2,1)S(1)}, u32[]{:S(2)}, u32[]{:S(2)}) async-start(bf16[128,64,128]{2,1,0:T(8,128)(2,1)} %bitcast.9), calls=%async_computation | async-start | bytes 4194304 | tf_op jit(solution)/shard_map/all_to_all | solution.py:364
  37.5 13.3 %copy-start.8 = (s32[16,6]{0,1:T(8,128)S(1)}, s32[16,6]{0,1:T(8,128)}, u32[]{:S(2)}) copy-start(s32[16,6]{0,1:T(8,128)} %param.16) | copy-start | bytes 1156
  37.5 13.3 %copy-start.9 = (f32[16,6]{0,1:T(8,128)S(1)}, f32[16,6]{0,1:T(8,128)}, u32[]{:S(2)}) copy-start(f32[16,6]{0,1:T(8,128)} %param.17) | copy-start | bytes 1156
  43.7 19.5 %collective-permute-start.3 = (f32[16,40,128]{2,1,0:T(8,128)S(1)}, f32[16,40,128]{2,1,0:T(8,128)S(1)}, u32[]{:S(2)}, u32[]{:S(2)}) collective-permute-start(f32[16,40,128]{2,1,0:T(8,128)S(1)} %tile_sums.1.o_ref), channel_id=1, source_target_pairs={{1,0},{2,1},{3,2},{4,3},{5,4},{6,5},{7,6},{8,7},{9,8},{10,9},{11,1... | collective-permute-start | bytes 983048 | tf_op jit(solution)/shard_map/ppermute | solution.py:352
  50.8 20.7 %collective-permute-start.2 = (f32[16,40,128]{2,1,0:T(8,128)S(1)}, f32[16,40,128]{2,1,0:T(8,128)S(1)}, u32[]{:S(2)}, u32[]{:S(2)}) collective-permute-start(f32[16,40,128]{2,1,0:T(8,128)S(1)} %tile_sums.1.o_ref), channel_id=1, source_target_pairs={{0,1},{1,2},{2,3},{3,4},{4,5},{5,6},{6,7},{7,8},{8,9},{9,10},{10,1... | collective-permute-start | bytes 983048 | tf_op jit(solution)/shard_map/ppermute | solution.py:351

commit v2 on v1

v2 whole, which is shorter than its diff:
```python
import functools

import jax
import jax.numpy as jnp
from jax import lax
from jax.experimental import pallas as pl
from jax.experimental.pallas import tpu as pltpu
from jax.sharding import PartitionSpec as P

NS_ITERS = 5
LANES = 128
SUB = 8


def call(kernel, name, out_shape, flops, traffic, vmem=24, **kw):
    return pl.pallas_call(
        kernel,
        name=name,
        out_shape=out_shape,
        cost_estimate=pl.CostEstimate(flops=flops, bytes_accessed=traffic, transcendentals=0),
        compiler_params=pltpu.CompilerParams(vmem_limit_bytes=vmem << 20),
        **kw,
    )


def parity():
    return lax.rem(lax.axis_index("lat"), 2)


def edge_rows(prior, north):
    groups, sub, lon = prior.shape

    def kernel(q_ref, v_ref, first_ref, second_ref, north_ref, rows_ref, sem):
        odd = parity()
        copies = [
            pltpu.make_async_copy(q_ref.at[:, (sub - 1) * side, :], rows_ref.at[k], sem.at[k])
            for k, side in enumerate((1 - odd, odd))
        ]
        courant = pltpu.make_async_copy(v_ref, north_ref, sem.at[2])
        courant.start()
        for copy in copies:
            copy.start()
        courant.wait()
        v = jnp.broadcast_to(north_ref[sub - 1 : sub, :], (16, lon))
        high = v.astype(jnp.bfloat16).astype(jnp.float32)
        row = lax.broadcasted_iota(jnp.int32, (16, lon), 0)
        parts = jnp.where(row == 0, high, jnp.where(row == 1, v - high, 0.0)).astype(jnp.bfloat16)
        for k, ref in enumerate((first_ref, second_ref)):
            copies[k].wait()
            ref[0:groups, :] = rows_ref[k].astype(jnp.bfloat16)
            ref[groups : groups + 16, :] = parts

    out = jax.ShapeDtypeStruct((groups + 16, lon), jnp.bfloat16)
    vmem = pl.BlockSpec(memory_space=pltpu.VMEM)
    return call(
        kernel,
        "edge_rows",
        (out, out),
        groups * lon * 2,
        groups * lon * 12,
        vmem=52,
        in_specs=[pl.BlockSpec(memory_space=pl.ANY)] * 2,
        out_specs=(vmem, vmem),
        scratch_shapes=[
            pltpu.VMEM((sub, lon), jnp.float32),
            pltpu.VMEM((2, groups, lon), jnp.float32),
            pltpu.SemaphoreType.DMA((3,)),
        ],
    )(prior, north)


def advect(prior, zonal, north, first_rows, second_rows, members, channels):
    sub, lon = zonal.shape
    blocks = lon // LANES
    width = channels * sub
    edges = members * channels
    chunks = 4
    chunk = lon * members // chunks
    starts = (0, members // 8, members // 2)
    ends = starts[1:] + (members,)

    def kernel(
        q_hbm, u_ref, v_ref, ra_ref, rb_ref, out_ref,
        q_ref, coef_ref, halo_ref, adv_ref, rows_ref, sent_ref, in_sem, out_sem,
    ):
        def copy_in(group, b):
            some = pl.ds(starts[group], ends[group] - starts[group])
            return pltpu.make_async_copy(
                q_hbm.at[some, :, pl.ds(b * LANES, LANES)],
                q_ref.at[b, some, pl.ds(sub, width)],
                in_sem.at[group, b],
            )

        for group in range(len(starts)):
            for b in range(blocks):
                copy_in(group, b).start()

        odd = parity()
        u, v = u_ref[...], v_ref[...]
        row = lax.broadcasted_iota(jnp.int32, (sub, lon), 0)
        below = [ref[edges : edges + 16, :].astype(jnp.float32) for ref in (ra_ref, rb_ref)]
        below = jnp.where(odd == 1, below[0], below[1])
        below = jnp.broadcast_to(below[0:1] + below[1:2], (sub, lon))
        v_south = jnp.where(row == 0, below, pltpu.roll(v, 1, 0))
        u_west = pltpu.roll(u, 1, 1)
        vp, vn = jnp.maximum(v, 0.0), jnp.minimum(v, 0.0)
        vps, vns = jnp.maximum(v_south, 0.0), jnp.minimum(v_south, 0.0)
        coefs = (
            1.0 - jnp.maximum(u, 0.0) + jnp.minimum(u_west, 0.0) - vp + vns,
            -jnp.minimum(u, 0.0),
            jnp.maximum(u_west, 0.0),
            -vn,
            vps,
        )
        for k, coef in enumerate(coefs):
            for b in range(blocks):
                coef_ref[k, b] = coef[:, b * LANES : (b + 1) * LANES]
        lane = lax.broadcasted_iota(jnp.int32, (sub, LANES), 1)
        line = lax.broadcasted_iota(jnp.int32, (sub, LANES), 0)
        start = channels - lax.rem(lax.axis_index("lat"), channels)

        def stencil(member, slot):
            at = pl.ds(pl.multiple_of(member * channels, channels), channels)
            for k, ref in enumerate((ra_ref, rb_ref)):
                halo = ref[at, :].astype(jnp.float32)
                for b in range(blocks):
                    halo_ref[slot, k, b] = halo[:, b * LANES : (b + 1) * LANES]
            coef = [[coef_ref[k, b] for b in range(blocks)] for k in range(5)]
            for p in range(channels):
                c = lax.rem(start + p, channels)
                base = pl.multiple_of((c + 1) * sub, sub)
                q = [q_ref[b, member, pl.ds(base, sub), :] for b in range(blocks)]
                east = [pltpu.roll(x, LANES - 1, 1) for x in q]
                west = [pltpu.roll(x, 1, 1) for x in q]
                for b in range(blocks):
                    q_east = jnp.where(lane == LANES - 1, east[(b + 1) % blocks], east[b])
                    q_west = jnp.where(lane == 0, west[b - 1], west[b])
                    q_north = q_ref[b, member, pl.ds(base + 1, sub), :]
                    q_south = q_ref[b, member, pl.ds(base - 1, sub), :]
                    halo_south = halo_ref[slot, 1 - odd, b, pl.ds(c, 1), :]
                    halo_north = halo_ref[slot, odd, b, pl.ds(c, 1), :]
                    q_south = jnp.where(line == 0, halo_south, q_south)
                    q_north = jnp.where(line == sub - 1, halo_north, q_north)
                    adv_ref[slot, b, p * sub : (p + 1) * sub, :] = (
                        q[b] * coef[0][b]
                        + q_east * coef[1][b]
                        + q_west * coef[2][b]
                        + q_north * coef[3][b]
                        + q_south * coef[4][b]
                    )

        def flush(member, slot):
            for b in range(blocks):
                first = b * LANES * members + member
                rows_ref[pl.ds(first, LANES, stride=members), :] = adv_ref[slot, b].T

        @pl.loop(0, members // 2)
        def _(pair):
            for group, first in enumerate(starts):

                @pl.when(pair == first // 2)
                def _():
                    for b in range(blocks):
                        copy_in(group, b).wait()

            member = pair * 2
            stencil(member, 0)
            flush(lax.rem(member + members - 1, members), 1)
            stencil(member + 1, 1)
            flush(member, 0)

        flush(members - 1, 1)

        copies = []
        for i in range(chunks):
            at = pl.ds(i * chunk, chunk)

            @pl.loop(0, chunk // 512)
            def _(j):
                part = pl.ds(pl.multiple_of(i * chunk + j * 512, 512), 512)
                sent_ref[part, :] = rows_ref[part, :].astype(jnp.bfloat16)

            copies.append(pltpu.make_async_copy(sent_ref.at[at], out_ref.at[at], out_sem.at[i]))
            copies[-1].start()
        for copy in copies:
            copy.wait()

    cells = members * channels * sub * lon
    vmem = pl.BlockSpec(memory_space=pltpu.VMEM)
    hbm = pl.BlockSpec(memory_space=pl.ANY)
    return call(
        kernel,
        "advect",
        jax.ShapeDtypeStruct((lon * members, width), jnp.bfloat16),
        cells * 10,
        cells * 6,
        vmem=52,
        in_specs=[hbm] + [vmem] * 4,
        out_specs=hbm,
        scratch_shapes=[
            pltpu.VMEM((blocks, members, width + 2 * sub, LANES), jnp.float32),
            pltpu.VMEM((5, blocks, sub, LANES), jnp.float32),
            pltpu.VMEM((2, 2, blocks, channels, LANES), jnp.float32),
            pltpu.VMEM((2, blocks, width, LANES), jnp.float32),
            pltpu.VMEM((lon * members, width), jnp.float32),
            pltpu.VMEM((lon * members, width), jnp.bfloat16),
            pltpu.SemaphoreType.DMA((len(starts), blocks)),
            pltpu.SemaphoreType.DMA((chunks,)),
        ],
    )(prior, zonal, north, first_rows, second_rows)


def tile_sums(perturb, innovation, inverse_error_variance, obs_count):
    tiles, members, cap = perturb.shape
    half = members // 2
    parts = 4
    per_part = tiles // parts

    def kernel(count_ref, p_ref, inn_ref, iev_ref, out_ref, held_ref, sem):
        copies = [
            pltpu.make_async_copy(
                p_ref.at[pl.ds(i * per_part, per_part)],
                held_ref.at[pl.ds(i * per_part, per_part)],
                sem.at[i],
            )
            for i in range(parts)
        ]
        for copy in copies:
            copy.start()
        slot = lax.broadcasted_iota(jnp.int32, (1, cap), 1)
        for tile in range(tiles):
            if tile % per_part == 0:
                copies[tile // per_part].wait()
            valid = slot < count_ref[tile]
            iev = iev_ref[tile : tile + 1, :]
            weight = jnp.where(valid, iev, 0.0)
            drive = jnp.where(valid, iev * inn_ref[tile : tile + 1, :], 0.0)
            weight = jnp.broadcast_to(weight, (16, cap)).astype(jnp.bfloat16)
            drive = jnp.broadcast_to(drive, (16, cap)).astype(jnp.bfloat16)
            p = held_ref[tile]
            left = jnp.concatenate(
                [p[i * 16 : (i + 1) * 16] * weight for i in range(members // 16)] + [drive], axis=0
            )
            sums = lax.dot_general(
                left, p, (((1,), (1,)), ((), ())), preferred_element_type=jnp.float32
            )
            out_ref[tile, 0:half, :] = jnp.concatenate([sums[0:half], sums[half:members]], axis=1)
            last = sums[members : members + SUB]
            out_ref[tile, half : half + SUB, :] = jnp.concatenate([last, last], axis=1)

    vmem = pl.BlockSpec(memory_space=pltpu.VMEM)
    return call(
        kernel,
        "tile_sums",
        jax.ShapeDtypeStruct((tiles, half + SUB, 2 * members), jnp.float32),
        2 * tiles * members * (members + 16) * cap,
        tiles * members * cap * 2,
        vmem=50,
        in_specs=[
            pl.BlockSpec(memory_space=pltpu.SMEM),
            pl.BlockSpec(memory_space=pl.ANY),
            vmem,
            vmem,
        ],
        out_specs=vmem,
        scratch_shapes=[
            pltpu.VMEM((tiles, members, cap), jnp.bfloat16),
            pltpu.SemaphoreType.DMA((parts,)),
        ],
    )(obs_count, perturb, innovation, inverse_error_variance)


def transform(own, first, second, neighbours, localization):
    tiles, packed, lanes = own.shape
    members = lanes // 2
    half = members // 2
    neigh = neighbours.shape[1]
    dot = functools.partial(
        jnp.dot, precision=lax.Precision.HIGHEST, preferred_element_type=jnp.float32
    )

    def kernel(nb_ref, loc_ref, o_ref, a_ref, b_ref, out_ref, win_ref, cur_ref, inv_ref, mid_ref):
        odd = parity()
        win_ref[tiles : 2 * tiles] = o_ref[...]
        win_ref[pl.ds((1 - odd) * 2 * tiles, tiles)] = a_ref[...]
        win_ref[pl.ds(odd * 2 * tiles, tiles)] = b_ref[...]
        row = lax.broadcasted_iota(jnp.int32, (members, members), 0)
        col = lax.broadcasted_iota(jnp.int32, (members, members), 1)
        eye = (row == col).astype(jnp.float32)
        drives, scales = [], []
        for t in range(tiles):
            total = loc_ref[t, 0] * win_ref[nb_ref[t, 0]]
            for n in range(1, neigh):
                total = total + loc_ref[t, n] * win_ref[nb_ref[t, n]]
            curvature = (members - 1.0) * eye + jnp.concatenate(
                [total[0:half, 0:members], total[0:half, members:]], axis=0
            )
            drives.append(total[half : half + SUB, 0:members])
            square = jnp.sum(curvature * curvature, axis=0, keepdims=True)
            scale = jnp.sqrt(jnp.sum(square, axis=1, keepdims=True))
            scales.append(scale)
            cur_ref[t] = curvature / scale
        for step in range(NS_ITERS):
            for t in range(tiles):
                product = cur_ref[t] if step == 0 else dot(inv_ref[t], cur_ref[t])
                mid_ref[t] = 1.5 * eye - 0.5 * product
            for t in range(tiles):
                middle = mid_ref[t]
                if step < NS_ITERS - 1:
                    cur_ref[t] = dot(cur_ref[t], middle)
                inv_ref[t] = middle if step == 0 else dot(middle, inv_ref[t])
        for t in range(tiles):
            flipped = inv_ref[t].T
            half_step = dot(drives[t], flipped)
            mean_part = dot(half_step, flipped)[0:1] / scales[t]
            weights = jnp.sqrt((members - 1.0) / scales[t]) * flipped + mean_part
            rest = (1.0 - jnp.sum(weights, axis=1, keepdims=True)) * (1.0 / members)
            weights = weights + rest
            high = weights.astype(jnp.bfloat16).astype(jnp.float32)
            out_ref[t] = jnp.concatenate([high, weights - high], axis=1).astype(jnp.bfloat16)

    cube = pltpu.VMEM((tiles, members, members), jnp.float32)
    vmem = pl.BlockSpec(memory_space=pltpu.VMEM)
    smem = pl.BlockSpec(memory_space=pltpu.SMEM)
    return call(
        kernel,
        "transform",
        jax.ShapeDtypeStruct((tiles, members, lanes), jnp.bfloat16),
        2 * tiles * members**3 * 72,
        tiles * packed * lanes * 12,
        in_specs=[smem, smem, vmem, vmem, vmem],
        out_specs=vmem,
        scratch_shapes=[pltpu.VMEM((3 * tiles, packed, lanes), jnp.float32), cube, cube, cube],
    )(neighbours, localization, own, first, second)


def analyse(arrived, weights, mem_count, lat_count, lon_strip):
    sources, rows, lanes = arrived.shape
    members_dev = rows // lon_strip
    tiles, members, _ = weights.shape
    bands = lat_count // tiles
    group = lanes // SUB
    halves = lat_count // group
    per_member = group * halves * lon_strip
    chunks = members // SUB
    chunk_rows = SUB * per_member

    def kernel(a_ref, w_ref, out_ref, product_ref, rows_ref, sem):
        @pl.loop(0, lon_strip)
        def _(x):
            at = pl.ds(pl.multiple_of(x * members_dev, members_dev), members_dev)
            for g in range(tiles):
                block = jnp.concatenate(
                    [
                        jnp.concatenate(
                            [a_ref[m * lat_count + g * bands + b, at, :] for m in range(mem_count)],
                            axis=0,
                        )
                        for b in range(bands)
                    ],
                    axis=1,
                )
                product = jnp.dot(
                    w_ref[g],
                    jnp.concatenate([block, block], axis=0),
                    preferred_element_type=jnp.float32,
                )
                for b in range(bands):
                    product_ref[x, g * bands + b] = product[:, b * lanes : (b + 1) * lanes]

        place = lax.broadcasted_iota(jnp.int32, (SUB, lanes), 1) // SUB

        def copy_out(j):
            at = pl.ds(pl.multiple_of(j * chunk_rows, chunk_rows), chunk_rows)
            return pltpu.make_async_copy(rows_ref.at[at], out_ref.at[at], sem.at[j])

        @pl.loop(0, chunks)
        def _(j):
            at = pl.ds(pl.multiple_of(j * SUB, SUB), SUB)
            for x in range(lon_strip):
                for half in range(halves):
                    held = [product_ref[x, half * group + b, at, :] for b in range(group)]
                    step = 1
                    while step < group:
                        odd = (place // step) % 2 == 1
                        held = [
                            jnp.where(odd, held[(r + step) % group], held[r]) for r in range(group)
                        ]
                        step *= 2
                    for c in range(group):
                        row = pltpu.roll(held[(-c) % group], (lanes - c * SUB) % lanes, 1)
                        first = j * chunk_rows + (c * halves + half) * lon_strip + x
                        rows_ref[pl.ds(first, SUB, stride=per_member), :] = row
            copy_out(j).start()

        @pl.loop(0, chunks)
        def _(j):
            copy_out(j).wait()

    vmem = pl.BlockSpec(memory_space=pltpu.VMEM)
    return call(
        kernel,
        "analyse",
        jax.ShapeDtypeStruct((members * per_member, lanes), jnp.float32),
        2 * tiles * members * 2 * members * bands * lanes * lon_strip,
        members * per_member * lanes * 6,
        in_specs=[vmem, vmem],
        out_specs=pl.BlockSpec(memory_space=pl.ANY),
        scratch_shapes=[
            pltpu.VMEM((lon_strip, lat_count, members, lanes), jnp.float32),
            pltpu.VMEM((members * per_member, lanes), jnp.float32),
            pltpu.SemaphoreType.DMA((chunks,)),
        ],
    )(arrived, weights)


def per_device(
    prior_member_stack,
    zonal_stability_ratio,
    meridional_stability_ratio,
    obs_perturb,
    innovation,
    inverse_error_variance,
    obs_count,
    neighbours,
    localization,
):
    members_dev, channels, row_count, lon_count = prior_member_stack.shape
    mem_count, lat_count = lax.axis_size("mem"), lax.axis_size("lat")
    devices = mem_count * lat_count
    lon_strip = lon_count // devices
    members = members_dev * mem_count

    first_rows, second_rows = edge_rows(
        prior_member_stack.reshape(members_dev * channels, row_count, lon_count),
        meridional_stability_ratio,
    )

    def swap(first, count, ring):
        pairs = [(i, (i + 1) % count) for i in range(first, count if ring else count - 1, 2)]
        return pairs + [(j, i) for i, j in pairs]

    first_rows = lax.ppermute(first_rows, "lat", swap(0, lat_count, False))
    second_rows = lax.ppermute(second_rows, "lat", swap(1, lat_count, False))

    sums = tile_sums(obs_perturb, innovation, inverse_error_variance, obs_count)
    first_rows, second_rows, sums = lax.optimization_barrier((first_rows, second_rows, sums))
    both = ("mem", "lat")
    first_sums = lax.ppermute(sums, both, swap(0, devices, True))
    second_sums = lax.ppermute(sums, both, swap(1, devices, True))

    sent = advect(
        prior_member_stack.reshape(members_dev, channels * row_count, lon_count),
        zonal_stability_ratio,
        meridional_stability_ratio,
        first_rows,
        second_rows,
        members_dev,
        channels,
    )
    sent = sent.reshape(devices, lon_strip * members_dev, channels * row_count)
    sent, first_sums, second_sums = lax.optimization_barrier((sent, first_sums, second_sums))
    arrived = lax.all_to_all(sent, both, split_axis=0, concat_axis=0, tiled=True)
    weights = transform(sums, first_sums, second_sums, neighbours, localization)
    rows = analyse(arrived, weights, mem_count, lat_count, lon_strip)
    halves = lat_count * row_count // LANES
    out = rows.reshape(members, channels, halves, lon_strip, LANES)
    out = jnp.transpose(out, (0, 1, 3, 2, 4))
    return out.reshape(members, channels, lon_strip, lat_count * row_count)


def solution(mesh):
    in_specs = (
        P("mem", None, "lat", None),
        P("lat", None),
        P("lat", None),
        P(("mem", "lat"), None, None),
        P(("mem", "lat"), None),
        P(("mem", "lat"), None),
        P(("mem", "lat")),
        P(("mem", "lat"), None),
        P(("mem", "lat"), None),
    )
    out_specs = P(None, None, ("mem", "lat"), None)
    return jax.shard_map(
        per_device, mesh=mesh, in_specs=in_specs, out_specs=out_specs, check_vma=False
    )
```

time: 87.7 us -> 70.3 us (0.80)
  starting transfers between devices: 26.6 us -> 17.4 us
  local copies, waits for them, and re-layouts: 4.42 us -> 0.97 us
  Pallas kernels: 31.7 us -> 28.6 us
  waiting for transfers between devices: 24.5 us -> 22.4 us
    ppermute x4, waiting for transfers between devices: 24.5 us -> 0.01 us  [the longest x1 0.01 us: per_device(): second_rows = lax.ppermute(second_rows, 'lat', swap(1, lat_count, False))]
    all_to_all x1, waiting for transfers between devices: 0.01 us -> 22.4 us  [per_device(): lax.all_to_all(sent, both, split_axis=0, concat_axis=0, tiled=True)]
    all_to_all x1, starting transfers between devices: 16.9 us -> 7.55 us  [per_device(): lax.all_to_all(sent, both, split_axis=0, concat_axis=0, tiled=True)]
    unnamed x22 -> x16, local copies, waits for them, and re-layouts: 4.42 us -> 0.97 us
    pallas_call x1, Pallas kernels: 8.25 us -> 4.99 us  [analyse(): call(kernel, 'analyse', jax.ShapeDtypeStruct((members * per_member, lanes...]
  transfers between devices with their start and end apart: 5 -> 5, of which waited for: 3 -> 1; matrix products, arithmetic and copies ran while one was open for 0% -> 0% of each run, Pallas kernels for 16% -> 32%
where the time goes in v2:
time: 70.3 us; the launch traced here: 69.7 us
  Pallas kernels  28.6 us (41%)
  waiting for transfers between devices  22.4 us (32%)
  starting transfers between devices  17.4 us (25%)
  local copies, waits for them, and re-layouts  0.97 us (1%)
    all_to_all x1, waiting for transfers between devices, per_device(): lax.all_to_all(sent, both, split_axis=0, concat_axis=0, tiled=True)  22.4 us
    ppermute x1, starting transfers between devices, per_device(): second_sums = lax.ppermute(sums, both, swap(1, devices, True))  9.06 us
    pallas_call x1, Pallas kernels, advect(): call(kernel, 'advect', jax.ShapeDtypeStruct((lon * members, width), jnp.b...  8.89 us
    pallas_call x1, Pallas kernels, transform(): call(kernel, 'transform', jax.ShapeDtypeStruct((tiles, members, lanes), j...  7.64 us
    all_to_all x1, starting transfers between devices, per_device(): lax.all_to_all(sent, both, split_axis=0, concat_axis=0, tiled=True)  7.55 us
    pallas_call x1, Pallas kernels, tile_sums(): call(kernel, 'tile_sums', jax.ShapeDtypeStruct((tiles, half + SUB, 2 * me...  5.77 us
    pallas_call x1, Pallas kernels, analyse(): call(kernel, 'analyse', jax.ShapeDtypeStruct((members * per_member, lanes...  4.99 us
  transfers between devices with their start and end apart: 5, of which 1 were waited for; matrix products, arithmetic and copies ran while one was open for 0% of the time, Pallas kernels for 32%

profile of v2, /device:TPU:0, one launch (start us, length us, event | category | flops | bytes accessed | tf_op | source)
XLA Modules:
  0.0 69.7 jit_solution(9589302100082587195)
XLA Ops:
  0.0 0.0 copy-start.1
  0.0 0.0 copy-start
  0.0 0.0 copy-start.2
  0.0 0.8 %copy-done.2 = f32[8,512]{1,0:T(8,128)S(1)} copy-done((f32[8,512]{1,0:T(8,128)S(1)}, f32[8,512]{1,0:T(8,128)}, u32[]{:S(2)}) %copy-start.2) | copy-done | bytes 16408
  0.8 0.0 copy-start.4
  0.8 1.3 %edge_rows.1 = (bf16[272,512]{1,0:T(8,128)(2,1)S(1)}, bf16[272,512]{1,0:T(8,128)(2,1)S(1)}) custom-call(f32[256,8,512]{2,1,0:T(8,128)} %bitcast.8, f32[8,512]{1,0:T(8,128)S(1)} %copy-done.2), custom_call_target="tpu_custom_call" | custom-call | flops 262144 | bytes 1572864 | tf_op jit(solution)/shard_map/edge_rows/pallas_call | solution.py:55
  2.1 0.1 collective-permute-start
  2.2 0.0 copy-start.3
  2.2 0.7 collective-permute-start.1
  2.9 0.0 copy-done.1
  2.9 0.0 copy-done
  2.9 0.0 copy-done.4
  2.9 5.8 %tile_sums.1.o_ref = f32[16,40,128]{2,1,0:T(8,128)S(1)} custom-call(s32[16]{0:T(128)S(1)} %copy-done.4, bf16[16,64,4096]{2,1,0:T(8,128)(2,1)} %p_ref.1, f32[16,4096]{1,0:T(8,128)S(1)} %copy-done, f32[16,4096]{1,0:T(8,128)S(1)} %copy-done.1), custom_call_target="tpu_custom_call" | custom-call | flops 671088640 | bytes 8388608 | tf_op jit(solution)/shard_map/tile_sums/pallas_call | solution.py:252
  8.7 0.0 collective-permute-done.ra_ref
  8.7 0.0 collective-permute-done.1.rb_ref
  8.7 9.1 %collective-permute-start.3 = (f32[16,40,128]{2,1,0:T(8,128)S(1)}, f32[16,40,128]{2,1,0:T(8,128)S(1)}, u32[]{:S(2)}, u32[]{:S(2)}) collective-permute-start(f32[16,40,128]{2,1,0:T(8,128)S(1)} %tile_sums.1.o_ref), channel_id=1, source_target_pairs={{1,2},{3,4},{5,6},{7,8},{9,10},{11,12},{13,14},{15,16},{17,18},{19... | collective-permute-start | bytes 983048 | tf_op jit(solution)/shard_map/ppermute | solution.py:450
  17.8 0.0 collective-permute-start.2
  17.8 0.0 copy-done.3
  17.8 0.0 copy-start.5
  17.8 0.0 copy-start.6
  17.8 8.9 %advect.1 = bf16[8192,128]{1,0:T(8,128)(2,1)} custom-call(f32[16,128,512]{2,1,0:T(8,128)} %bitcast.9, f32[8,512]{1,0:T(8,128)S(1)} %copy-done.3, f32[8,512]{1,0:T(8,128)S(1)} %copy-done.2, bf16[272,512]{1,0:T(8,128)(2,1)S(1)} %collective-permute-done.ra_ref, bf16[272,512]{1,0:T(8,128)(2,1)S(1)} %collective-permute-done.1.rb_ref), custom_call_target="tpu_custom_call" | custom-call | flops 10485760 | bytes 6291456 | tf_op jit(solution)/shard_map/advect/pallas_call | solution.py:191
  26.7 0.0 collective-permute-done.3.b_ref
  26.7 0.0 collective-permute-done.2.a_ref
  26.7 7.5 %all-to-all-start = ((bf16[128,64,128]{2,1,0:T(8,128)(2,1)}), bf16[128,64,128]{2,1,0:T(8,128)(2,1)S(1)}, u32[]{:S(2)}, u32[]{:S(2)}) async-start(bf16[128,64,128]{2,1,0:T(8,128)(2,1)} %bitcast.10), calls=%async_computation | async-start | bytes 4194304 | tf_op jit(solution)/shard_map/all_to_all | solution.py:463
  34.3 0.0 copy-done.5
  34.3 0.1 copy.10.nb_ref
  34.4 0.0 copy-done.6
  34.4 0.1 copy.11.loc_ref
  34.4 7.6 %transform.1.w_ref = bf16[16,64,128]{2,1,0:T(8,128)(2,1)S(1)} custom-call(s32[16,6]{1,0:T(8,128)S(1)} %copy.10.nb_ref, f32[16,6]{1,0:T(8,128)S(1)} %copy.11.loc_ref, f32[16,40,128]{2,1,0:T(8,128)S(1)} %tile_sums.1.o_ref, f32[16,40,128]{2,1,0:T(8,128)S(1)} %collective-permute-done.2.a_ref, f32[16,40,128]{2,1,0:T(8,128)S(1)} %collective-permute-done.3.b_ref), custom_call_target="tpu_custom_call" | custom-call | flops 603979776 | bytes 983040 | tf_op jit(solution)/shard_map/transform/pallas_call | solution.py:325
  42.1 22.4 %all-to-all-done.a_ref = bf16[128,64,128]{2,1,0:T(8,128)(2,1)S(1)} async-done(((bf16[128,64,128]{2,1,0:T(8,128)(2,1)}), bf16[128,64,128]{2,1,0:T(8,128)(2,1)S(1)}, u32[]{:S(2)}, u32[]{:S(2)}) %all-to-all-start) | async-done | bytes 2097184 | tf_op jit(solution)/shard_map/all_to_all | solution.py:463
  64.5 5.0 %analyse.1 = f32[8192,128]{1,0:T(8,128)} custom-call(bf16[128,64,128]{2,1,0:T(8,128)(2,1)S(1)} %all-to-all-done.a_ref, bf16[16,64,128]{2,1,0:T(8,128)(2,1)S(1)} %transform.1.w_ref), custom_call_target="tpu_custom_call" | custom-call | flops 268435456 | bytes 6291456 | tf_op jit(solution)/shard_map/analyse/pallas_call | solution.py:401
Async XLA Ops:
  0.0 2.9 %copy-start.1 = (f32[16,4096]{1,0:T(8,128)S(1)}, f32[16,4096]{1,0:T(8,128)}, u32[]{:S(2)}) copy-start(f32[16,4096]{1,0:T(8,128)} %iev_ref.1) | copy-start | bytes 786436
  0.0 2.9 %copy-start = (f32[16,4096]{1,0:T(8,128)S(1)}, f32[16,4096]{1,0:T(8,128)}, u32[]{:S(2)}) copy-start(f32[16,4096]{1,0:T(8,128)} %inn_ref.1) | copy-start | bytes 786436
  0.0 0.8 %copy-start.2 = (f32[8,512]{1,0:T(8,128)S(1)}, f32[8,512]{1,0:T(8,128)}, u32[]{:S(2)}) copy-start(f32[8,512]{1,0:T(8,128)} %v_ref.3) | copy-start | bytes 49156
  0.8 2.1 %copy-start.4 = (s32[16]{0:T(128)S(1)}, s32[16]{0:T(128)}, u32[]{:S(2)}) copy-start(s32[16]{0:T(128)} %count_ref.1) | copy-start | bytes 196
  2.1 6.6 %collective-permute-start = (bf16[272,512]{1,0:T(8,128)(2,1)S(1)}, bf16[272,512]{1,0:T(8,128)(2,1)S(1)}, u32[]{:S(2)}, u32[]{:S(2)}) collective-permute-start(bf16[272,512]{1,0:T(8,128)(2,1)S(1)} %get-tuple-element.13), channel_id=1, source_target_pairs={{0,1},{2,3},{4,5},{6,7},{8,9},{10,11},{12,13},{14,15},{16,17},{18,... | collective-permute-start | bytes 835592 | tf_op jit(solution)/shard_map/ppermute | solution.py:443
  2.2 15.6 %copy-start.3 = (f32[8,512]{1,0:T(8,128)S(1)}, f32[8,512]{1,0:T(8,128)}, u32[]{:S(2)}) copy-start(f32[8,512]{1,0:T(8,128)} %u_ref.1) | copy-start | bytes 49156
  2.2 6.5 %collective-permute-start.1 = (bf16[272,512]{1,0:T(8,128)(2,1)S(1)}, bf16[272,512]{1,0:T(8,128)(2,1)S(1)}, u32[]{:S(2)}, u32[]{:S(2)}) collective-permute-start(bf16[272,512]{1,0:T(8,128)(2,1)S(1)} %get-tuple-element.14), channel_id=1, source_target_pairs={{1,2},{3,4},{5,6},{7,8},{9,10},{11,12},{13,14},{15,16},{17,18},{19... | collective-permute-start | bytes 835592 | tf_op jit(solution)/shard_map/ppermute | solution.py:444
  8.7 18.0 %collective-permute-start.3 = (f32[16,40,128]{2,1,0:T(8,128)S(1)}, f32[16,40,128]{2,1,0:T(8,128)S(1)}, u32[]{:S(2)}, u32[]{:S(2)}) collective-permute-start(f32[16,40,128]{2,1,0:T(8,128)S(1)} %tile_sums.1.o_ref), channel_id=1, source_target_pairs={{1,2},{3,4},{5,6},{7,8},{9,10},{11,12},{13,14},{15,16},{17,18},{19... | collective-permute-start | bytes 983048 | tf_op jit(solution)/shard_map/ppermute | solution.py:450
  17.8 8.9 %collective-permute-start.2 = (f32[16,40,128]{2,1,0:T(8,128)S(1)}, f32[16,40,128]{2,1,0:T(8,128)S(1)}, u32[]{:S(2)}, u32[]{:S(2)}) collective-permute-start(f32[16,40,128]{2,1,0:T(8,128)S(1)} %tile_sums.1.o_ref), channel_id=1, source_target_pairs={{0,1},{2,3},{4,5},{6,7},{8,9},{10,11},{12,13},{14,15},{16,17},{18,... | collective-permute-start | bytes 983048 | tf_op jit(solution)/shard_map/ppermute | solution.py:449
  17.8 16.5 %copy-start.5 = (s32[16,6]{0,1:T(8,128)S(1)}, s32[16,6]{0,1:T(8,128)}, u32[]{:S(2)}) copy-start(s32[16,6]{0,1:T(8,128)} %param.16) | copy-start | bytes 1156
  17.8 16.6 %copy-start.6 = (f32[16,6]{0,1:T(8,128)S(1)}, f32[16,6]{0,1:T(8,128)}, u32[]{:S(2)}) copy-start(f32[16,6]{0,1:T(8,128)} %param.17) | copy-start | bytes 1156
  26.7 37.8 %all-to-all-start = ((bf16[128,64,128]{2,1,0:T(8,128)(2,1)}), bf16[128,64,128]{2,1,0:T(8,128)(2,1)S(1)}, u32[]{:S(2)}, u32[]{:S(2)}) async-start(bf16[128,64,128]{2,1,0:T(8,128)(2,1)} %bitcast.10), calls=%async_computation | async-start | bytes 4194304 | tf_op jit(solution)/shard_map/all_to_all | solution.py:463

commit v3 on v2

--- a/solution.py
+++ b/solution.py
@@ -74,9 +74,9 @@
     blocks = lon // LANES
     width = channels * sub
     edges = members * channels
-    chunks = 4
-    chunk = lon * members // chunks
-    starts = (0, members // 8, members // 2)
+    chunk = LANES * members
+    pitch = members + SUB
+    starts = (0, members // 4, members // 2)
     ends = starts[1:] + (members,)
 
     def kernel(
@@ -141,7 +141,7 @@
                     halo_north = halo_ref[slot, odd, b, pl.ds(c, 1), :]
                     q_south = jnp.where(line == 0, halo_south, q_south)
                     q_north = jnp.where(line == sub - 1, halo_north, q_north)
-                    adv_ref[slot, b, p * sub : (p + 1) * sub, :] = (
+                    adv_ref[member, b, p * sub : (p + 1) * sub, :] = (
                         q[b] * coef[0][b]
                         + q_east * coef[1][b]
                         + q_west * coef[2][b]
@@ -149,38 +149,29 @@
                         + q_south * coef[4][b]
                     )
 
-        def flush(member, slot):
-            for b in range(blocks):
-                first = b * LANES * members + member
-                rows_ref[pl.ds(first, LANES, stride=members), :] = adv_ref[slot, b].T
-
-        @pl.loop(0, members // 2)
-        def _(pair):
+        @pl.loop(0, members // 4)
+        def _(four):
             for group, first in enumerate(starts):
 
-                @pl.when(pair == first // 2)
+                @pl.when(four == first // 4)
                 def _():
                     for b in range(blocks):
                         copy_in(group, b).wait()
 
-            member = pair * 2
-            stencil(member, 0)
-            flush(lax.rem(member + members - 1, members), 1)
-            stencil(member + 1, 1)
-            flush(member, 0)
-
-        flush(members - 1, 1)
+            for k in range(4):
+                stencil(four * 4 + k, k)
 
         copies = []
-        for i in range(chunks):
-            at = pl.ds(i * chunk, chunk)
-
-            @pl.loop(0, chunk // 512)
-            def _(j):
-                part = pl.ds(pl.multiple_of(i * chunk + j * 512, 512), 512)
-                sent_ref[part, :] = rows_ref[part, :].astype(jnp.bfloat16)
-
-            copies.append(pltpu.make_async_copy(sent_ref.at[at], out_ref.at[at], out_sem.at[i]))
+        for b in range(blocks):
+            for member in range(members):
+                at = pl.ds(member, LANES, stride=pitch)
+                rows_ref[b % 2, at, :] = adv_ref[member, b].T
+            for x in range(LANES):
+                to = pl.ds(b * chunk + x * members, members)
+                at = pl.ds(x * pitch, members)
+                sent_ref[to, :] = rows_ref[b % 2, at, :].astype(jnp.bfloat16)
+            at = pl.ds(b * chunk, chunk)
+            copies.append(pltpu.make_async_copy(sent_ref.at[at], out_ref.at[at], out_sem.at[b]))
             copies[-1].start()
         for copy in copies:
             copy.wait()
@@ -200,12 +191,12 @@
         scratch_shapes=[
             pltpu.VMEM((blocks, members, width + 2 * sub, LANES), jnp.float32),
             pltpu.VMEM((5, blocks, sub, LANES), jnp.float32),
-            pltpu.VMEM((2, 2, blocks, channels, LANES), jnp.float32),
-            pltpu.VMEM((2, blocks, width, LANES), jnp.float32),
-            pltpu.VMEM((lon * members, width), jnp.float32),
+            pltpu.VMEM((4, 2, blocks, channels, LANES), jnp.float32),
+            pltpu.VMEM((members, blocks, width, LANES), jnp.float32),
+            pltpu.VMEM((2, LANES * pitch, width), jnp.float32),
             pltpu.VMEM((lon * members, width), jnp.bfloat16),
             pltpu.SemaphoreType.DMA((len(starts), blocks)),
-            pltpu.SemaphoreType.DMA((chunks,)),
+            pltpu.SemaphoreType.DMA((blocks,)),
         ],
     )(prior, zonal, north, first_rows, second_rows)
 
@@ -343,7 +334,7 @@
     halves = lat_count // group
     per_member = group * halves * lon_strip
     chunks = members // SUB
-    chunk_rows = SUB * per_member
+    pitch = per_member + SUB
 
     def kernel(a_ref, w_ref, out_ref, product_ref, rows_ref, sem):
         @pl.loop(0, lon_strip)
@@ -368,15 +359,17 @@
                 for b in range(bands):
                     product_ref[x, g * bands + b] = product[:, b * lanes : (b + 1) * lanes]
 
+        flat_ref = rows_ref.reshape(members * pitch, lanes)
         place = lax.broadcasted_iota(jnp.int32, (SUB, lanes), 1) // SUB
 
         def copy_out(j):
-            at = pl.ds(pl.multiple_of(j * chunk_rows, chunk_rows), chunk_rows)
-            return pltpu.make_async_copy(rows_ref.at[at], out_ref.at[at], sem.at[j])
-
-        @pl.loop(0, chunks)
-        def _(j):
-            at = pl.ds(pl.multiple_of(j * SUB, SUB), SUB)
+            at = pl.ds(j * SUB, SUB)
+            return pltpu.make_async_copy(
+                rows_ref.at[at, pl.ds(0, per_member)], out_ref.at[at], sem.at[j]
+            )
+
+        for j in range(chunks):
+            at = pl.ds(j * SUB, SUB)
             for x in range(lon_strip):
                 for half in range(halves):
                     held = [product_ref[x, half * group + b, at, :] for b in range(group)]
@@ -389,26 +382,25 @@
                         step *= 2
                     for c in range(group):
                         row = pltpu.roll(held[(-c) % group], (lanes - c * SUB) % lanes, 1)
-                        first = j * chunk_rows + (c * halves + half) * lon_strip + x
-                        rows_ref[pl.ds(first, SUB, stride=per_member), :] = row
+                        first = j * SUB * pitch + (c * halves + half) * lon_strip + x
+                        flat_ref[pl.ds(first, SUB, stride=pitch), :] = row
             copy_out(j).start()
 
-        @pl.loop(0, chunks)
-        def _(j):
+        for j in range(chunks):
             copy_out(j).wait()
 
     vmem = pl.BlockSpec(memory_space=pltpu.VMEM)
     return call(
         kernel,
         "analyse",
-        jax.ShapeDtypeStruct((members * per_member, lanes), jnp.float32),
+        jax.ShapeDtypeStruct((members, per_member, lanes), jnp.float32),
         2 * tiles * members * 2 * members * bands * lanes * lon_strip,
         members * per_member * lanes * 6,
         in_specs=[vmem, vmem],
         out_specs=pl.BlockSpec(memory_space=pl.ANY),
         scratch_shapes=[
             pltpu.VMEM((lon_strip, lat_count, members, lanes), jnp.float32),
-            pltpu.VMEM((members * per_member, lanes), jnp.float32),
+            pltpu.VMEM((members, pitch, lanes), jnp.float32),
             pltpu.SemaphoreType.DMA((chunks,)),
         ],
     )(arrived, weights)

time: 70.3 us -> 67.2 us (0.956)
  Pallas kernels: 28.6 us -> 25.3 us
    pallas_call x1, Pallas kernels: 8.89 us -> 7.06 us  [advect(): call(kernel, 'advect', jax.ShapeDtypeStruct((lon * members, width), jnp.b...]
    pallas_call x1, Pallas kernels: 4.99 us -> 3.54 us  [analyse(): call(kernel, 'analyse', jax.ShapeDtypeStruct((members, per_member, lanes)...]
  transfers between devices with their start and end apart: 5 -> 5, of which waited for: 1 -> 1; matrix products, arithmetic and copies ran while one was open for 0% -> 0% of each run, Pallas kernels for 32% -> 31%
where the time goes in v3:
time: 67.2 us; the launch traced here: 66.6 us
  Pallas kernels  25.3 us (38%)
  waiting for transfers between devices  22.4 us (33%)
  starting transfers between devices  17.5 us (26%)
  local copies, waits for them, and re-layouts  0.97 us (1%)
    all_to_all x1, waiting for transfers between devices, per_device(): lax.all_to_all(sent, both, split_axis=0, concat_axis=0, tiled=True)  22.4 us
    ppermute x1, starting transfers between devices, per_device(): second_sums = lax.ppermute(sums, both, swap(1, devices, True))  9.06 us
    all_to_all x1, starting transfers between devices, per_device(): lax.all_to_all(sent, both, split_axis=0, concat_axis=0, tiled=True)  7.72 us
    pallas_call x1, Pallas kernels, transform(): call(kernel, 'transform', jax.ShapeDtypeStruct((tiles, members, lanes), j...  7.64 us
    pallas_call x1, Pallas kernels, advect(): call(kernel, 'advect', jax.ShapeDtypeStruct((lon * members, width), jnp.b...  7.06 us
    pallas_call x1, Pallas kernels, tile_sums(): call(kernel, 'tile_sums', jax.ShapeDtypeStruct((tiles, half + SUB, 2 * me...  5.77 us
    pallas_call x1, Pallas kernels, analyse(): call(kernel, 'analyse', jax.ShapeDtypeStruct((members, per_member, lanes)...  3.54 us
  transfers between devices with their start and end apart: 5, of which 1 were waited for; matrix products, arithmetic and copies ran while one was open for 0% of the time, Pallas kernels for 31%

profile of v3, /device:TPU:0, one launch (start us, length us, event | category | flops | bytes accessed | tf_op | source)
XLA Modules:
  0.0 66.6 jit_solution(12597049518752689374)
XLA Ops:
  0.0 0.0 copy-start.1
  0.0 0.0 copy-start
  0.0 0.0 copy-start.2
  0.0 0.8 %copy-done.2 = f32[8,512]{1,0:T(8,128)S(1)} copy-done((f32[8,512]{1,0:T(8,128)S(1)}, f32[8,512]{1,0:T(8,128)}, u32[]{:S(2)}) %copy-start.2) | copy-done | bytes 16408
  0.8 0.0 copy-start.4
  0.8 1.3 %edge_rows.1 = (bf16[272,512]{1,0:T(8,128)(2,1)S(1)}, bf16[272,512]{1,0:T(8,128)(2,1)S(1)}) custom-call(f32[256,8,512]{2,1,0:T(8,128)} %bitcast.8, f32[8,512]{1,0:T(8,128)S(1)} %copy-done.2), custom_call_target="tpu_custom_call" | custom-call | flops 262144 | bytes 1572864 | tf_op jit(solution)/shard_map/edge_rows/pallas_call | solution.py:55
  2.1 0.1 collective-permute-start
  2.2 0.0 copy-start.3
  2.2 0.7 %collective-permute-start.1 = (bf16[272,512]{1,0:T(8,128)(2,1)S(1)}, bf16[272,512]{1,0:T(8,128)(2,1)S(1)}, u32[]{:S(2)}, u32[]{:S(2)}) collective-permute-start(bf16[272,512]{1,0:T(8,128)(2,1)S(1)} %get-tuple-element.14), channel_id=1, source_target_pairs={{1,2},{3,4},{5,6},{7,8},{9,10},{11,12},{13,14},{15,16},{17,18},{19... | collective-permute-start | bytes 835592 | tf_op jit(solution)/shard_map/ppermute | solution.py:436
  2.9 0.0 copy-done.1
  2.9 0.0 copy-done
  2.9 0.0 copy-done.4
  2.9 5.8 %tile_sums.1.o_ref = f32[16,40,128]{2,1,0:T(8,128)S(1)} custom-call(s32[16]{0:T(128)S(1)} %copy-done.4, bf16[16,64,4096]{2,1,0:T(8,128)(2,1)} %p_ref.1, f32[16,4096]{1,0:T(8,128)S(1)} %copy-done, f32[16,4096]{1,0:T(8,128)S(1)} %copy-done.1), custom_call_target="tpu_custom_call" | custom-call | flops 671088640 | bytes 8388608 | tf_op jit(solution)/shard_map/tile_sums/pallas_call | solution.py:243
  8.7 0.0 collective-permute-done.ra_ref
  8.7 0.0 collective-permute-done.1.rb_ref
  8.7 9.1 %collective-permute-start.3 = (f32[16,40,128]{2,1,0:T(8,128)S(1)}, f32[16,40,128]{2,1,0:T(8,128)S(1)}, u32[]{:S(2)}, u32[]{:S(2)}) collective-permute-start(f32[16,40,128]{2,1,0:T(8,128)S(1)} %tile_sums.1.o_ref), channel_id=1, source_target_pairs={{1,2},{3,4},{5,6},{7,8},{9,10},{11,12},{13,14},{15,16},{17,18},{19... | collective-permute-start | bytes 983048 | tf_op jit(solution)/shard_map/ppermute | solution.py:442
  17.8 0.0 collective-permute-start.2
  17.8 0.0 copy-done.3
  17.8 0.0 copy-start.5
  17.8 0.0 copy-start.6
  17.8 7.1 %advect.1 = bf16[8192,128]{1,0:T(8,128)(2,1)} custom-call(f32[16,128,512]{2,1,0:T(8,128)} %bitcast.9, f32[8,512]{1,0:T(8,128)S(1)} %copy-done.3, f32[8,512]{1,0:T(8,128)S(1)} %copy-done.2, bf16[272,512]{1,0:T(8,128)(2,1)S(1)} %collective-permute-done.ra_ref, bf16[272,512]{1,0:T(8,128)(2,1)S(1)} %collective-permute-done.1.rb_ref), custom_call_target="tpu_custom_call" | custom-call | flops 10485760 | bytes 6291456 | tf_op jit(solution)/shard_map/advect/pallas_call | solution.py:182
  24.9 0.0 collective-permute-done.3.b_ref
  24.9 0.0 collective-permute-done.2.a_ref
  24.9 7.7 %all-to-all-start = ((bf16[128,64,128]{2,1,0:T(8,128)(2,1)}), bf16[128,64,128]{2,1,0:T(8,128)(2,1)S(1)}, u32[]{:S(2)}, u32[]{:S(2)}) async-start(bf16[128,64,128]{2,1,0:T(8,128)(2,1)} %bitcast.10), calls=%async_computation | async-start | bytes 4194304 | tf_op jit(solution)/shard_map/all_to_all | solution.py:455
  32.6 0.0 copy-done.5
  32.6 0.1 copy.10.nb_ref
  32.7 0.0 copy-done.6
  32.7 0.1 copy.11.loc_ref
  32.8 7.6 %transform.1.w_ref = bf16[16,64,128]{2,1,0:T(8,128)(2,1)S(1)} custom-call(s32[16,6]{1,0:T(8,128)S(1)} %copy.10.nb_ref, f32[16,6]{1,0:T(8,128)S(1)} %copy.11.loc_ref, f32[16,40,128]{2,1,0:T(8,128)S(1)} %tile_sums.1.o_ref, f32[16,40,128]{2,1,0:T(8,128)S(1)} %collective-permute-done.2.a_ref, f32[16,40,128]{2,1,0:T(8,128)S(1)} %collective-permute-done.3.b_ref), custom_call_target="tpu_custom_call" | custom-call | flops 603979776 | bytes 983040 | tf_op jit(solution)/shard_map/transform/pallas_call | solution.py:316
  40.4 22.4 %all-to-all-done.a_ref = bf16[128,64,128]{2,1,0:T(8,128)(2,1)S(1)} async-done(((bf16[128,64,128]{2,1,0:T(8,128)(2,1)}), bf16[128,64,128]{2,1,0:T(8,128)(2,1)S(1)}, u32[]{:S(2)}, u32[]{:S(2)}) %all-to-all-start) | async-done | bytes 2097184 | tf_op jit(solution)/shard_map/all_to_all | solution.py:455
  62.9 3.5 %analyse.1 = f32[64,128,128]{2,1,0:T(8,128)} custom-call(bf16[128,64,128]{2,1,0:T(8,128)(2,1)S(1)} %all-to-all-done.a_ref, bf16[16,64,128]{2,1,0:T(8,128)(2,1)S(1)} %transform.1.w_ref), custom_call_target="tpu_custom_call" | custom-call | flops 268435456 | bytes 6291456 | tf_op jit(solution)/shard_map/analyse/pallas_call | solution.py:393
Async XLA Ops:
  0.0 2.9 %copy-start.1 = (f32[16,4096]{1,0:T(8,128)S(1)}, f32[16,4096]{1,0:T(8,128)}, u32[]{:S(2)}) copy-start(f32[16,4096]{1,0:T(8,128)} %iev_ref.1) | copy-start | bytes 786436
  0.0 2.9 %copy-start = (f32[16,4096]{1,0:T(8,128)S(1)}, f32[16,4096]{1,0:T(8,128)}, u32[]{:S(2)}) copy-start(f32[16,4096]{1,0:T(8,128)} %inn_ref.1) | copy-start | bytes 786436
  0.0 0.8 %copy-start.2 = (f32[8,512]{1,0:T(8,128)S(1)}, f32[8,512]{1,0:T(8,128)}, u32[]{:S(2)}) copy-start(f32[8,512]{1,0:T(8,128)} %v_ref.3) | copy-start | bytes 49156
  0.8 2.1 %copy-start.4 = (s32[16]{0:T(128)S(1)}, s32[16]{0:T(128)}, u32[]{:S(2)}) copy-start(s32[16]{0:T(128)} %count_ref.1) | copy-start | bytes 196
  2.1 6.6 %collective-permute-start = (bf16[272,512]{1,0:T(8,128)(2,1)S(1)}, bf16[272,512]{1,0:T(8,128)(2,1)S(1)}, u32[]{:S(2)}, u32[]{:S(2)}) collective-permute-start(bf16[272,512]{1,0:T(8,128)(2,1)S(1)} %get-tuple-element.13), channel_id=1, source_target_pairs={{0,1},{2,3},{4,5},{6,7},{8,9},{10,11},{12,13},{14,15},{16,17},{18,... | collective-permute-start | bytes 835592 | tf_op jit(solution)/shard_map/ppermute | solution.py:435
  2.2 15.6 %copy-start.3 = (f32[8,512]{1,0:T(8,128)S(1)}, f32[8,512]{1,0:T(8,128)}, u32[]{:S(2)}) copy-start(f32[8,512]{1,0:T(8,128)} %u_ref.1) | copy-start | bytes 49156
  2.2 6.5 %collective-permute-start.1 = (bf16[272,512]{1,0:T(8,128)(2,1)S(1)}, bf16[272,512]{1,0:T(8,128)(2,1)S(1)}, u32[]{:S(2)}, u32[]{:S(2)}) collective-permute-start(bf16[272,512]{1,0:T(8,128)(2,1)S(1)} %get-tuple-element.14), channel_id=1, source_target_pairs={{1,2},{3,4},{5,6},{7,8},{9,10},{11,12},{13,14},{15,16},{17,18},{19... | collective-permute-start | bytes 835592 | tf_op jit(solution)/shard_map/ppermute | solution.py:436
  8.7 16.1 %collective-permute-start.3 = (f32[16,40,128]{2,1,0:T(8,128)S(1)}, f32[16,40,128]{2,1,0:T(8,128)S(1)}, u32[]{:S(2)}, u32[]{:S(2)}) collective-permute-start(f32[16,40,128]{2,1,0:T(8,128)S(1)} %tile_sums.1.o_ref), channel_id=1, source_target_pairs={{1,2},{3,4},{5,6},{7,8},{9,10},{11,12},{13,14},{15,16},{17,18},{19... | collective-permute-start | bytes 983048 | tf_op jit(solution)/shard_map/ppermute | solution.py:442
  17.8 7.1 %collective-permute-start.2 = (f32[16,40,128]{2,1,0:T(8,128)S(1)}, f32[16,40,128]{2,1,0:T(8,128)S(1)}, u32[]{:S(2)}, u32[]{:S(2)}) collective-permute-start(f32[16,40,128]{2,1,0:T(8,128)S(1)} %tile_sums.1.o_ref), channel_id=1, source_target_pairs={{0,1},{2,3},{4,5},{6,7},{8,9},{10,11},{12,13},{14,15},{16,17},{18,... | collective-permute-start | bytes 983048 | tf_op jit(solution)/shard_map/ppermute | solution.py:441
  17.8 14.8 %copy-start.5 = (s32[16,6]{0,1:T(8,128)S(1)}, s32[16,6]{0,1:T(8,128)}, u32[]{:S(2)}) copy-start(s32[16,6]{0,1:T(8,128)} %param.16) | copy-start | bytes 1156
  17.8 14.9 %copy-start.6 = (f32[16,6]{0,1:T(8,128)S(1)}, f32[16,6]{0,1:T(8,128)}, u32[]{:S(2)}) copy-start(f32[16,6]{0,1:T(8,128)} %param.17) | copy-start | bytes 1156
  24.9 38.0 %all-to-all-start = ((bf16[128,64,128]{2,1,0:T(8,128)(2,1)}), bf16[128,64,128]{2,1,0:T(8,128)(2,1)S(1)}, u32[]{:S(2)}, u32[]{:S(2)}) async-start(bf16[128,64,128]{2,1,0:T(8,128)(2,1)} %bitcast.10), calls=%async_computation | async-start | bytes 4194304 | tf_op jit(solution)/shard_map/all_to_all | solution.py:455

commit v4 on v3

--- a/solution.py
+++ b/solution.py
@@ -193,7 +193,7 @@
             pltpu.VMEM((5, blocks, sub, LANES), jnp.float32),
             pltpu.VMEM((4, 2, blocks, channels, LANES), jnp.float32),
             pltpu.VMEM((members, blocks, width, LANES), jnp.float32),
-            pltpu.VMEM((2, LANES * pitch, width), jnp.float32),
+            pltpu.VMEM((2, (LANES + 1) * pitch, width), jnp.float32),
             pltpu.VMEM((lon * members, width), jnp.bfloat16),
             pltpu.SemaphoreType.DMA((len(starts), blocks)),
             pltpu.SemaphoreType.DMA((blocks,)),
@@ -337,9 +337,8 @@
     pitch = per_member + SUB
 
     def kernel(a_ref, w_ref, out_ref, product_ref, rows_ref, sem):
-        @pl.loop(0, lon_strip)
-        def _(x):
-            at = pl.ds(pl.multiple_of(x * members_dev, members_dev), members_dev)
+        for x in range(lon_strip):
+            at = pl.ds(x * members_dev, members_dev)
             for g in range(tiles):
                 block = jnp.concatenate(
                     [
@@ -359,7 +358,7 @@
                 for b in range(bands):
                     product_ref[x, g * bands + b] = product[:, b * lanes : (b + 1) * lanes]
 
-        flat_ref = rows_ref.reshape(members * pitch, lanes)
+        flat_ref = rows_ref.reshape((members + 1) * pitch, lanes)
         place = lax.broadcasted_iota(jnp.int32, (SUB, lanes), 1) // SUB
 
         def copy_out(j):
@@ -400,7 +399,7 @@
         out_specs=pl.BlockSpec(memory_space=pl.ANY),
         scratch_shapes=[
             pltpu.VMEM((lon_strip, lat_count, members, lanes), jnp.float32),
-            pltpu.VMEM((members, pitch, lanes), jnp.float32),
+            pltpu.VMEM((members + 1, pitch, lanes), jnp.float32),
             pltpu.SemaphoreType.DMA((chunks,)),
         ],
     )(arrived, weights)

time: 67.2 us -> 66.9 us (level)
  no operation moved by 1% of the time
where the time goes in v4:
time: 66.9 us; the launch traced here: 66.2 us
  Pallas kernels  25 us (37%)
  waiting for transfers between devices  22.4 us (33%)
  starting transfers between devices  17.6 us (26%)
  local copies, waits for them, and re-layouts  0.97 us (1%)
    all_to_all x1, waiting for transfers between devices, per_device(): lax.all_to_all(sent, both, split_axis=0, concat_axis=0, tiled=True)  22.4 us
    ppermute x1, starting transfers between devices, per_device(): second_sums = lax.ppermute(sums, both, swap(1, devices, True))  9.06 us
    all_to_all x1, starting transfers between devices, per_device(): lax.all_to_all(sent, both, split_axis=0, concat_axis=0, tiled=True)  7.73 us
    pallas_call x1, Pallas kernels, transform(): call(kernel, 'transform', jax.ShapeDtypeStruct((tiles, members, lanes), j...  7.63 us
    pallas_call x1, Pallas kernels, advect(): call(kernel, 'advect', jax.ShapeDtypeStruct((lon * members, width), jnp.b...  7.05 us
    pallas_call x1, Pallas kernels, tile_sums(): call(kernel, 'tile_sums', jax.ShapeDtypeStruct((tiles, half + SUB, 2 * me...  5.77 us
    pallas_call x1, Pallas kernels, analyse(): call(kernel, 'analyse', jax.ShapeDtypeStruct((members, per_member, lanes)...  3.19 us
  transfers between devices with their start and end apart: 5, of which 1 were waited for; matrix products, arithmetic and copies ran while one was open for 0% of the time, Pallas kernels for 31%

profile of v4, /device:TPU:0, one launch (start us, length us, event | category | flops | bytes accessed | tf_op | source)
XLA Modules:
  0.0 66.2 jit_solution(1604984185879612641)
XLA Ops:
  0.0 0.0 copy-start.1
  0.0 0.0 copy-start
  0.0 0.0 copy-start.2
  0.0 0.8 %copy-done.2 = f32[8,512]{1,0:T(8,128)S(1)} copy-done((f32[8,512]{1,0:T(8,128)S(1)}, f32[8,512]{1,0:T(8,128)}, u32[]{:S(2)}) %copy-start.2) | copy-done | bytes 16408
  0.8 0.0 copy-start.4
  0.8 1.3 %edge_rows.1 = (bf16[272,512]{1,0:T(8,128)(2,1)S(1)}, bf16[272,512]{1,0:T(8,128)(2,1)S(1)}) custom-call(f32[256,8,512]{2,1,0:T(8,128)} %bitcast.8, f32[8,512]{1,0:T(8,128)S(1)} %copy-done.2), custom_call_target="tpu_custom_call" | custom-call | flops 262144 | bytes 1572864 | tf_op jit(solution)/shard_map/edge_rows/pallas_call | solution.py:55
  2.1 0.1 collective-permute-start
  2.2 0.0 copy-start.3
  2.2 0.7 %collective-permute-start.1 = (bf16[272,512]{1,0:T(8,128)(2,1)S(1)}, bf16[272,512]{1,0:T(8,128)(2,1)S(1)}, u32[]{:S(2)}, u32[]{:S(2)}) collective-permute-start(bf16[272,512]{1,0:T(8,128)(2,1)S(1)} %get-tuple-element.14), channel_id=1, source_target_pairs={{1,2},{3,4},{5,6},{7,8},{9,10},{11,12},{13,14},{15,16},{17,18},{19... | collective-permute-start | bytes 835592 | tf_op jit(solution)/shard_map/ppermute | solution.py:435
  2.9 0.0 copy-done.1
  2.9 0.0 copy-done
  2.9 0.0 copy-done.4
  2.9 5.8 %tile_sums.1.o_ref = f32[16,40,128]{2,1,0:T(8,128)S(1)} custom-call(s32[16]{0:T(128)S(1)} %copy-done.4, bf16[16,64,4096]{2,1,0:T(8,128)(2,1)} %p_ref.1, f32[16,4096]{1,0:T(8,128)S(1)} %copy-done, f32[16,4096]{1,0:T(8,128)S(1)} %copy-done.1), custom_call_target="tpu_custom_call" | custom-call | flops 671088640 | bytes 8388608 | tf_op jit(solution)/shard_map/tile_sums/pallas_call | solution.py:243
  8.7 0.0 collective-permute-done.ra_ref
  8.7 0.0 collective-permute-done.1.rb_ref
  8.7 9.1 %collective-permute-start.3 = (f32[16,40,128]{2,1,0:T(8,128)S(1)}, f32[16,40,128]{2,1,0:T(8,128)S(1)}, u32[]{:S(2)}, u32[]{:S(2)}) collective-permute-start(f32[16,40,128]{2,1,0:T(8,128)S(1)} %tile_sums.1.o_ref), channel_id=1, source_target_pairs={{1,2},{3,4},{5,6},{7,8},{9,10},{11,12},{13,14},{15,16},{17,18},{19... | collective-permute-start | bytes 983048 | tf_op jit(solution)/shard_map/ppermute | solution.py:441
  17.8 0.0 collective-permute-start.2
  17.8 0.0 copy-done.3
  17.8 0.0 copy-start.5
  17.8 0.0 copy-start.6
  17.8 7.0 %advect.1 = bf16[8192,128]{1,0:T(8,128)(2,1)} custom-call(f32[16,128,512]{2,1,0:T(8,128)} %bitcast.9, f32[8,512]{1,0:T(8,128)S(1)} %copy-done.3, f32[8,512]{1,0:T(8,128)S(1)} %copy-done.2, bf16[272,512]{1,0:T(8,128)(2,1)S(1)} %collective-permute-done.ra_ref, bf16[272,512]{1,0:T(8,128)(2,1)S(1)} %collective-permute-done.1.rb_ref), custom_call_target="tpu_custom_call" | custom-call | flops 10485760 | bytes 6291456 | tf_op jit(solution)/shard_map/advect/pallas_call | solution.py:182
  24.9 0.0 collective-permute-done.3.b_ref
  24.9 0.0 collective-permute-done.2.a_ref
  24.9 7.7 %all-to-all-start = ((bf16[128,64,128]{2,1,0:T(8,128)(2,1)}), bf16[128,64,128]{2,1,0:T(8,128)(2,1)S(1)}, u32[]{:S(2)}, u32[]{:S(2)}) async-start(bf16[128,64,128]{2,1,0:T(8,128)(2,1)} %bitcast.10), calls=%async_computation | async-start | bytes 4194304 | tf_op jit(solution)/shard_map/all_to_all | solution.py:454
  32.6 0.0 copy-done.5
  32.6 0.1 copy.10.nb_ref
  32.7 0.0 copy-done.6
  32.7 0.1 copy.11.loc_ref
  32.8 7.6 %transform.1.w_ref = bf16[16,64,128]{2,1,0:T(8,128)(2,1)S(1)} custom-call(s32[16,6]{1,0:T(8,128)S(1)} %copy.10.nb_ref, f32[16,6]{1,0:T(8,128)S(1)} %copy.11.loc_ref, f32[16,40,128]{2,1,0:T(8,128)S(1)} %tile_sums.1.o_ref, f32[16,40,128]{2,1,0:T(8,128)S(1)} %collective-permute-done.2.a_ref, f32[16,40,128]{2,1,0:T(8,128)S(1)} %collective-permute-done.3.b_ref), custom_call_target="tpu_custom_call" | custom-call | flops 603979776 | bytes 983040 | tf_op jit(solution)/shard_map/transform/pallas_call | solution.py:316
  40.4 22.4 %all-to-all-done.a_ref = bf16[128,64,128]{2,1,0:T(8,128)(2,1)S(1)} async-done(((bf16[128,64,128]{2,1,0:T(8,128)(2,1)}), bf16[128,64,128]{2,1,0:T(8,128)(2,1)S(1)}, u32[]{:S(2)}, u32[]{:S(2)}) %all-to-all-start) | async-done | bytes 2097184 | tf_op jit(solution)/shard_map/all_to_all | solution.py:454
  62.9 3.2 %analyse.1 = f32[64,128,128]{2,1,0:T(8,128)} custom-call(bf16[128,64,128]{2,1,0:T(8,128)(2,1)S(1)} %all-to-all-done.a_ref, bf16[16,64,128]{2,1,0:T(8,128)(2,1)S(1)} %transform.1.w_ref), custom_call_target="tpu_custom_call" | custom-call | flops 268435456 | bytes 6291456 | tf_op jit(solution)/shard_map/analyse/pallas_call | solution.py:392
Async XLA Ops:
  0.0 2.9 %copy-start.1 = (f32[16,4096]{1,0:T(8,128)S(1)}, f32[16,4096]{1,0:T(8,128)}, u32[]{:S(2)}) copy-start(f32[16,4096]{1,0:T(8,128)} %iev_ref.1) | copy-start | bytes 786436
  0.0 2.9 %copy-start = (f32[16,4096]{1,0:T(8,128)S(1)}, f32[16,4096]{1,0:T(8,128)}, u32[]{:S(2)}) copy-start(f32[16,4096]{1,0:T(8,128)} %inn_ref.1) | copy-start | bytes 786436
  0.0 0.8 %copy-start.2 = (f32[8,512]{1,0:T(8,128)S(1)}, f32[8,512]{1,0:T(8,128)}, u32[]{:S(2)}) copy-start(f32[8,512]{1,0:T(8,128)} %v_ref.3) | copy-start | bytes 49156
  0.8 2.1 %copy-start.4 = (s32[16]{0:T(128)S(1)}, s32[16]{0:T(128)}, u32[]{:S(2)}) copy-start(s32[16]{0:T(128)} %count_ref.1) | copy-start | bytes 196
  2.1 6.6 %collective-permute-start = (bf16[272,512]{1,0:T(8,128)(2,1)S(1)}, bf16[272,512]{1,0:T(8,128)(2,1)S(1)}, u32[]{:S(2)}, u32[]{:S(2)}) collective-permute-start(bf16[272,512]{1,0:T(8,128)(2,1)S(1)} %get-tuple-element.13), channel_id=1, source_target_pairs={{0,1},{2,3},{4,5},{6,7},{8,9},{10,11},{12,13},{14,15},{16,17},{18,... | collective-permute-start | bytes 835592 | tf_op jit(solution)/shard_map/ppermute | solution.py:434
  2.2 15.6 %copy-start.3 = (f32[8,512]{1,0:T(8,128)S(1)}, f32[8,512]{1,0:T(8,128)}, u32[]{:S(2)}) copy-start(f32[8,512]{1,0:T(8,128)} %u_ref.1) | copy-start | bytes 49156
  2.2 6.5 %collective-permute-start.1 = (bf16[272,512]{1,0:T(8,128)(2,1)S(1)}, bf16[272,512]{1,0:T(8,128)(2,1)S(1)}, u32[]{:S(2)}, u32[]{:S(2)}) collective-permute-start(bf16[272,512]{1,0:T(8,128)(2,1)S(1)} %get-tuple-element.14), channel_id=1, source_target_pairs={{1,2},{3,4},{5,6},{7,8},{9,10},{11,12},{13,14},{15,16},{17,18},{19... | collective-permute-start | bytes 835592 | tf_op jit(solution)/shard_map/ppermute | solution.py:435
  8.7 16.1 %collective-permute-start.3 = (f32[16,40,128]{2,1,0:T(8,128)S(1)}, f32[16,40,128]{2,1,0:T(8,128)S(1)}, u32[]{:S(2)}, u32[]{:S(2)}) collective-permute-start(f32[16,40,128]{2,1,0:T(8,128)S(1)} %tile_sums.1.o_ref), channel_id=1, source_target_pairs={{1,2},{3,4},{5,6},{7,8},{9,10},{11,12},{13,14},{15,16},{17,18},{19... | collective-permute-start | bytes 983048 | tf_op jit(solution)/shard_map/ppermute | solution.py:441
  17.8 7.1 %collective-permute-start.2 = (f32[16,40,128]{2,1,0:T(8,128)S(1)}, f32[16,40,128]{2,1,0:T(8,128)S(1)}, u32[]{:S(2)}, u32[]{:S(2)}) collective-permute-start(f32[16,40,128]{2,1,0:T(8,128)S(1)} %tile_sums.1.o_ref), channel_id=1, source_target_pairs={{0,1},{2,3},{4,5},{6,7},{8,9},{10,11},{12,13},{14,15},{16,17},{18,... | collective-permute-start | bytes 983048 | tf_op jit(solution)/shard_map/ppermute | solution.py:440
  17.8 14.8 %copy-start.5 = (s32[16,6]{0,1:T(8,128)S(1)}, s32[16,6]{0,1:T(8,128)}, u32[]{:S(2)}) copy-start(s32[16,6]{0,1:T(8,128)} %param.16) | copy-start | bytes 1156
  17.8 14.9 %copy-start.6 = (f32[16,6]{0,1:T(8,128)S(1)}, f32[16,6]{0,1:T(8,128)}, u32[]{:S(2)}) copy-start(f32[16,6]{0,1:T(8,128)} %param.17) | copy-start | bytes 1156
  24.9 38.0 %all-to-all-start = ((bf16[128,64,128]{2,1,0:T(8,128)(2,1)}), bf16[128,64,128]{2,1,0:T(8,128)(2,1)S(1)}, u32[]{:S(2)}, u32[]{:S(2)}) async-start(bf16[128,64,128]{2,1,0:T(8,128)(2,1)} %bitcast.10), calls=%async_computation | async-start | bytes 4194304 | tf_op jit(solution)/shard_map/all_to_all | solution.py:454

commit v5 on v4

--- a/solution.py
+++ b/solution.py
@@ -30,7 +30,7 @@
 def edge_rows(prior, north):
     groups, sub, lon = prior.shape
 
-    def kernel(q_ref, v_ref, first_ref, second_ref, north_ref, rows_ref, sem):
+    def kernel(q_ref, v_ref, first_ref, second_ref, north_ref, rows_ref, sent_ref, sem, out_sem):
         odd = parity()
         copies = [
             pltpu.make_async_copy(q_ref.at[:, (sub - 1) * side, :], rows_ref.at[k], sem.at[k])
@@ -45,26 +45,32 @@
         high = v.astype(jnp.bfloat16).astype(jnp.float32)
         row = lax.broadcasted_iota(jnp.int32, (16, lon), 0)
         parts = jnp.where(row == 0, high, jnp.where(row == 1, v - high, 0.0)).astype(jnp.bfloat16)
+        leaving = []
         for k, ref in enumerate((first_ref, second_ref)):
             copies[k].wait()
-            ref[0:groups, :] = rows_ref[k].astype(jnp.bfloat16)
-            ref[groups : groups + 16, :] = parts
+            sent_ref[k, 0:groups, :] = rows_ref[k].astype(jnp.bfloat16)
+            sent_ref[k, groups : groups + 16, :] = parts
+            leaving.append(pltpu.make_async_copy(sent_ref.at[k], ref, out_sem.at[k]))
+            leaving[k].start()
+        for copy in leaving:
+            copy.wait()
 
     out = jax.ShapeDtypeStruct((groups + 16, lon), jnp.bfloat16)
-    vmem = pl.BlockSpec(memory_space=pltpu.VMEM)
     return call(
         kernel,
         "edge_rows",
-        (out, out),
+        [out, out],
         groups * lon * 2,
         groups * lon * 12,
-        vmem=52,
+        vmem=54,
         in_specs=[pl.BlockSpec(memory_space=pl.ANY)] * 2,
-        out_specs=(vmem, vmem),
+        out_specs=[pl.BlockSpec(memory_space=pl.ANY)] * 2,
         scratch_shapes=[
             pltpu.VMEM((sub, lon), jnp.float32),
             pltpu.VMEM((2, groups, lon), jnp.float32),
+            pltpu.VMEM((2, groups + 16, lon), jnp.bfloat16),
             pltpu.SemaphoreType.DMA((3,)),
+            pltpu.SemaphoreType.DMA((2,)),
         ],
     )(prior, north)
 

time: 66.9 us -> 66.8 us (level)
  local copies, waits for them, and re-layouts: 0.97 us -> 0.2 us
  Pallas kernels: 25 us -> 25.7 us
    pallas_call x1, Pallas kernels: 1.32 us -> 2.11 us  [edge_rows(): call(kernel, 'edge_rows', [out, out], groups * lon * 2, groups * lon * 12...]
    unnamed x16, local copies, waits for them, and re-layouts: 0.97 us -> 0.2 us
where the time goes in v5:
time: 66.8 us; the launch traced here: 66.3 us
  Pallas kernels  25.7 us (38%)
  waiting for transfers between devices  22.4 us (34%)
  starting transfers between devices  17.6 us (26%)
    all_to_all x1, waiting for transfers between devices, per_device(): lax.all_to_all(sent, both, split_axis=0, concat_axis=0, tiled=True)  22.4 us
    ppermute x1, starting transfers between devices, per_device(): second_sums = lax.ppermute(sums, both, swap(1, devices, True))  9.06 us
    all_to_all x1, starting transfers between devices, per_device(): lax.all_to_all(sent, both, split_axis=0, concat_axis=0, tiled=True)  7.73 us
    pallas_call x1, Pallas kernels, transform(): call(kernel, 'transform', jax.ShapeDtypeStruct((tiles, members, lanes), j...  7.64 us
    pallas_call x1, Pallas kernels, advect(): call(kernel, 'advect', jax.ShapeDtypeStruct((lon * members, width), jnp.b...  7.04 us
    pallas_call x1, Pallas kernels, tile_sums(): call(kernel, 'tile_sums', jax.ShapeDtypeStruct((tiles, half + SUB, 2 * me...  5.77 us
    pallas_call x1, Pallas kernels, analyse(): call(kernel, 'analyse', jax.ShapeDtypeStruct((members, per_member, lanes)...  3.19 us
    pallas_call x1, Pallas kernels, edge_rows(): call(kernel, 'edge_rows', [out, out], groups * lon * 2, groups * lon * 12...  2.11 us
  transfers between devices with their start and end apart: 5, of which 1 were waited for; matrix products, arithmetic and copies ran while one was open for 0% of the time, Pallas kernels for 31%

profile of v5, /device:TPU:0, one launch (start us, length us, event | category | flops | bytes accessed | tf_op | source)
XLA Modules:
  0.0 66.3 jit_solution(14388381499379518351)
XLA Ops:
  0.0 0.0 copy-start.4
  0.0 0.0 copy-start.1
  0.0 0.0 copy-start
  0.0 2.1 %edge_rows.1 = (bf16[272,512]{1,0:T(8,128)(2,1)}, bf16[272,512]{1,0:T(8,128)(2,1)}) custom-call(f32[256,8,512]{2,1,0:T(8,128)} %bitcast.8, f32[8,512]{1,0:T(8,128)} %v_ref.3), custom_call_target="tpu_custom_call" | custom-call | flops 262144 | bytes 1572864 | tf_op jit(solution)/shard_map/edge_rows/pallas_call | solution.py:59
  2.1 0.1 collective-permute-start
  2.2 0.0 copy-start.2
  2.2 0.0 copy-start.3
  2.2 0.7 %collective-permute-start.1 = (bf16[272,512]{1,0:T(8,128)(2,1)}, bf16[272,512]{1,0:T(8,128)(2,1)S(1)}, u32[]{:S(2)}, u32[]{:S(2)}) collective-permute-start(bf16[272,512]{1,0:T(8,128)(2,1)} %get-tuple-element.14), channel_id=1, source_target_pairs={{1,2},{3,4},{5,6},{7,8},{9,10},{11,12},{13,14},{15,16},{17,18},{19... | collective-permute-start | bytes 835592 | tf_op jit(solution)/shard_map/ppermute | solution.py:441
  2.9 0.0 copy-done.4
  2.9 0.0 copy-done.1
  2.9 0.0 copy-done
  3.0 5.8 %tile_sums.1.o_ref = f32[16,40,128]{2,1,0:T(8,128)S(1)} custom-call(s32[16]{0:T(128)S(1)} %copy-done.4, bf16[16,64,4096]{2,1,0:T(8,128)(2,1)} %p_ref.1, f32[16,4096]{1,0:T(8,128)S(1)} %copy-done, f32[16,4096]{1,0:T(8,128)S(1)} %copy-done.1), custom_call_target="tpu_custom_call" | custom-call | flops 671088640 | bytes 8388608 | tf_op jit(solution)/shard_map/tile_sums/pallas_call | solution.py:249
  8.7 0.0 collective-permute-done.ra_ref
  8.7 0.0 collective-permute-done.1.rb_ref
  8.8 9.1 %collective-permute-start.3 = (f32[16,40,128]{2,1,0:T(8,128)S(1)}, f32[16,40,128]{2,1,0:T(8,128)S(1)}, u32[]{:S(2)}, u32[]{:S(2)}) collective-permute-start(f32[16,40,128]{2,1,0:T(8,128)S(1)} %tile_sums.1.o_ref), channel_id=1, source_target_pairs={{1,2},{3,4},{5,6},{7,8},{9,10},{11,12},{13,14},{15,16},{17,18},{19... | collective-permute-start | bytes 983048 | tf_op jit(solution)/shard_map/ppermute | solution.py:447
  17.8 0.0 collective-permute-start.2
  17.8 0.0 copy-done.2
  17.8 0.0 copy-done.3
  17.8 0.0 copy-start.5
  17.8 0.0 copy-start.6
  17.8 7.0 %advect.1 = bf16[8192,128]{1,0:T(8,128)(2,1)} custom-call(f32[16,128,512]{2,1,0:T(8,128)} %bitcast.9, f32[8,512]{1,0:T(8,128)S(1)} %copy-done.3, f32[8,512]{1,0:T(8,128)S(1)} %copy-done.2, bf16[272,512]{1,0:T(8,128)(2,1)S(1)} %collective-permute-done.ra_ref, bf16[272,512]{1,0:T(8,128)(2,1)S(1)} %collective-permute-done.1.rb_ref), custom_call_target="tpu_custom_call" | custom-call | flops 10485760 | bytes 6291456 | tf_op jit(solution)/shard_map/advect/pallas_call | solution.py:188
  24.9 0.0 collective-permute-done.3.b_ref
  24.9 0.0 collective-permute-done.2.a_ref
  24.9 7.7 %all-to-all-start = ((bf16[128,64,128]{2,1,0:T(8,128)(2,1)}), bf16[128,64,128]{2,1,0:T(8,128)(2,1)S(1)}, u32[]{:S(2)}, u32[]{:S(2)}) async-start(bf16[128,64,128]{2,1,0:T(8,128)(2,1)} %bitcast.10), calls=%async_computation | async-start | bytes 4194304 | tf_op jit(solution)/shard_map/all_to_all | solution.py:460
  32.7 0.0 copy-done.5
  32.7 0.1 copy.10.nb_ref
  32.7 0.0 copy-done.6
  32.8 0.1 copy.11.loc_ref
  32.8 7.6 %transform.1.w_ref = bf16[16,64,128]{2,1,0:T(8,128)(2,1)S(1)} custom-call(s32[16,6]{1,0:T(8,128)S(1)} %copy.10.nb_ref, f32[16,6]{1,0:T(8,128)S(1)} %copy.11.loc_ref, f32[16,40,128]{2,1,0:T(8,128)S(1)} %tile_sums.1.o_ref, f32[16,40,128]{2,1,0:T(8,128)S(1)} %collective-permute-done.2.a_ref, f32[16,40,128]{2,1,0:T(8,128)S(1)} %collective-permute-done.3.b_ref), custom_call_target="tpu_custom_call" | custom-call | flops 603979776 | bytes 983040 | tf_op jit(solution)/shard_map/transform/pallas_call | solution.py:322
  40.5 22.4 %all-to-all-done.a_ref = bf16[128,64,128]{2,1,0:T(8,128)(2,1)S(1)} async-done(((bf16[128,64,128]{2,1,0:T(8,128)(2,1)}), bf16[128,64,128]{2,1,0:T(8,128)(2,1)S(1)}, u32[]{:S(2)}, u32[]{:S(2)}) %all-to-all-start) | async-done | bytes 2097184 | tf_op jit(solution)/shard_map/all_to_all | solution.py:460
  62.9 3.2 %analyse.1 = f32[64,128,128]{2,1,0:T(8,128)} custom-call(bf16[128,64,128]{2,1,0:T(8,128)(2,1)S(1)} %all-to-all-done.a_ref, bf16[16,64,128]{2,1,0:T(8,128)(2,1)S(1)} %transform.1.w_ref), custom_call_target="tpu_custom_call" | custom-call | flops 268435456 | bytes 6291456 | tf_op jit(solution)/shard_map/analyse/pallas_call | solution.py:398
Async XLA Ops:
  0.0 2.9 %copy-start.4 = (s32[16]{0:T(128)S(1)}, s32[16]{0:T(128)}, u32[]{:S(2)}) copy-start(s32[16]{0:T(128)} %count_ref.1) | copy-start | bytes 196
  0.0 2.9 %copy-start.1 = (f32[16,4096]{1,0:T(8,128)S(1)}, f32[16,4096]{1,0:T(8,128)}, u32[]{:S(2)}) copy-start(f32[16,4096]{1,0:T(8,128)} %iev_ref.1) | copy-start | bytes 786436
  0.0 2.9 %copy-start = (f32[16,4096]{1,0:T(8,128)S(1)}, f32[16,4096]{1,0:T(8,128)}, u32[]{:S(2)}) copy-start(f32[16,4096]{1,0:T(8,128)} %inn_ref.1) | copy-start | bytes 786436
  2.1 6.6 %collective-permute-start = (bf16[272,512]{1,0:T(8,128)(2,1)}, bf16[272,512]{1,0:T(8,128)(2,1)S(1)}, u32[]{:S(2)}, u32[]{:S(2)}) collective-permute-start(bf16[272,512]{1,0:T(8,128)(2,1)} %get-tuple-element.13), channel_id=1, source_target_pairs={{0,1},{2,3},{4,5},{6,7},{8,9},{10,11},{12,13},{14,15},{16,17},{18,... | collective-permute-start | bytes 835592 | tf_op jit(solution)/shard_map/ppermute | solution.py:440
  2.2 15.6 %copy-start.2 = (f32[8,512]{1,0:T(8,128)S(1)}, f32[8,512]{1,0:T(8,128)}, u32[]{:S(2)}) copy-start(f32[8,512]{1,0:T(8,128)} %v_ref.3) | copy-start | bytes 49156
  2.2 15.6 %copy-start.3 = (f32[8,512]{1,0:T(8,128)S(1)}, f32[8,512]{1,0:T(8,128)}, u32[]{:S(2)}) copy-start(f32[8,512]{1,0:T(8,128)} %u_ref.1) | copy-start | bytes 49156
  2.2 6.5 %collective-permute-start.1 = (bf16[272,512]{1,0:T(8,128)(2,1)}, bf16[272,512]{1,0:T(8,128)(2,1)S(1)}, u32[]{:S(2)}, u32[]{:S(2)}) collective-permute-start(bf16[272,512]{1,0:T(8,128)(2,1)} %get-tuple-element.14), channel_id=1, source_target_pairs={{1,2},{3,4},{5,6},{7,8},{9,10},{11,12},{13,14},{15,16},{17,18},{19... | collective-permute-start | bytes 835592 | tf_op jit(solution)/shard_map/ppermute | solution.py:441
  8.8 16.1 %collective-permute-start.3 = (f32[16,40,128]{2,1,0:T(8,128)S(1)}, f32[16,40,128]{2,1,0:T(8,128)S(1)}, u32[]{:S(2)}, u32[]{:S(2)}) collective-permute-start(f32[16,40,128]{2,1,0:T(8,128)S(1)} %tile_sums.1.o_ref), channel_id=1, source_target_pairs={{1,2},{3,4},{5,6},{7,8},{9,10},{11,12},{13,14},{15,16},{17,18},{19... | collective-permute-start | bytes 983048 | tf_op jit(solution)/shard_map/ppermute | solution.py:447
  17.8 7.1 %collective-permute-start.2 = (f32[16,40,128]{2,1,0:T(8,128)S(1)}, f32[16,40,128]{2,1,0:T(8,128)S(1)}, u32[]{:S(2)}, u32[]{:S(2)}) collective-permute-start(f32[16,40,128]{2,1,0:T(8,128)S(1)} %tile_sums.1.o_ref), channel_id=1, source_target_pairs={{0,1},{2,3},{4,5},{6,7},{8,9},{10,11},{12,13},{14,15},{16,17},{18,... | collective-permute-start | bytes 983048 | tf_op jit(solution)/shard_map/ppermute | solution.py:446
  17.8 14.8 %copy-start.5 = (s32[16,6]{0,1:T(8,128)S(1)}, s32[16,6]{0,1:T(8,128)}, u32[]{:S(2)}) copy-start(s32[16,6]{0,1:T(8,128)} %param.16) | copy-start | bytes 1156
  17.8 14.9 %copy-start.6 = (f32[16,6]{0,1:T(8,128)S(1)}, f32[16,6]{0,1:T(8,128)}, u32[]{:S(2)}) copy-start(f32[16,6]{0,1:T(8,128)} %param.17) | copy-start | bytes 1156
  24.9 38.0 %all-to-all-start = ((bf16[128,64,128]{2,1,0:T(8,128)(2,1)}), bf16[128,64,128]{2,1,0:T(8,128)(2,1)S(1)}, u32[]{:S(2)}, u32[]{:S(2)}) async-start(bf16[128,64,128]{2,1,0:T(8,128)(2,1)} %bitcast.10), calls=%async_computation | async-start | bytes 4194304 | tf_op jit(solution)/shard_map/all_to_all | solution.py:460
